TPU v7x, 512 devices: a whole 4x8x8 slice. The times are simulated.
512 devices in a mesh: fsdp: 64 (over x, z, core), tensor: 8 (over y).
Axes of the slice: x: 4, y: 8, z: 8, core: 2. Of those that a mesh axis runs over, the one named last changes fastest.
Arguments:
- grads: bfloat16 [64, 1024, 1024], P('fsdp', 'tensor'), may hold values from -6 to 6
- row_counts: int32 [64], replicated, may hold values from 512 to 1024, as said below
- col_counts: int32 [64], replicated, may hold values from 512 to 1024, as said below
- old_left: bfloat16 [64, 1024, 1024], P('fsdp', 'tensor'), may hold values from -1 to 2
- old_right: bfloat16 [64, 1024, 1024], P('fsdp', 'tensor'), may hold values from -1 to 2
Outputs:
- new_left: bfloat16 [64, 1024, 1024], P('fsdp', 'tensor')
- new_right: bfloat16 [64, 1024, 1024], P('fsdp', 'tensor')
Inputs may be any that keep to these rules, and one draw needn't show every extreme that they name: `row_counts`: a multiple of 128; some block has all 1024 rows. `col_counts`: a multiple of 128; some block has all 1024 columns.
All inputs are finite; a program needn't handle non-finite values.
Results may differ from a plain program's by a relative error of at most 0.0068.
Values may be sent and summed in bfloat16 or wider, within the bound.
A program may use at most 128 MiB of HBM per device.

v0:
```python
import jax
import jax.numpy as jnp
from jax import lax
from jax.sharding import PartitionSpec as P

TRAINERS = 4


def from_behind(block, axis, distance):
    devices = range(lax.axis_size(axis))
    route = [(i - distance, i) for i in devices if i - distance in devices]
    return lax.ppermute(block, axis, route)


def shortened(array):
    return jax.tree.map(lambda a: a.astype(jnp.bfloat16) if a.dtype == jnp.float32 else a, array)


def product_nt(left, right):
    return lax.dot_general(
        left,
        right,
        (((1,), (1,)), ((), ())),
        precision=lax.Precision.HIGHEST,
        preferred_element_type=jnp.float32,
    )


def refresh_one(stat, basis, owner_flag):
    power = (
        jnp.dot(stat, basis, preferred_element_type=jnp.float32) + basis.astype(jnp.float32)
    ).astype(jnp.bfloat16)
    gram = lax.dot_general(
        power, power, (((0,), (0,)), ((), ())), preferred_element_type=jnp.float32
    )
    total = gram.shape[0]
    identity = jnp.eye(total, dtype=jnp.float32)
    gram = jnp.where(owner_flag, gram, identity)
    width = min(128, total)
    count = total // width
    panels = []
    for step in range(count):
        low = step * width
        column = gram[low:, low : low + width]
        for prior in range(step):
            offset = low - prior * width
            earlier = panels[prior]
            column = column - product_nt(earlier[offset:], earlier[offset : offset + width])
        diag_block = jnp.linalg.cholesky(column[:width])
        if total - low > width:
            below = lax.linalg.triangular_solve(
                diag_block, column[width:], left_side=False, lower=True, transpose_a=True
            )
            panels.append(jnp.concatenate([diag_block, below], axis=0))
        else:
            panels.append(diag_block)
    pieces = []
    for step in range(count):
        low = step * width
        rhs = power[:, low : low + width].astype(jnp.float32)
        for prior in range(step):
            offset = low - prior * width
            rhs = rhs - product_nt(pieces[prior], panels[prior][offset : offset + width])
        diag_block = panels[step][:width]
        pieces.append(
            lax.linalg.triangular_solve(
                diag_block, rhs, left_side=False, lower=True, transpose_a=True
            )
        )
    solved = jnp.concatenate(pieces, axis=1)
    return solved.astype(jnp.bfloat16)


def body(grads, row_counts, col_counts, old_left, old_right):
    side = grads.shape[2]
    lanes = lax.axis_size("tensor")
    lane = lax.axis_index("tensor")
    block = lax.axis_index("fsdp")
    local_rows = grads.shape[1]
    row_ids = lane * local_rows + jnp.arange(local_rows, dtype=jnp.int32)
    col_ids = jnp.arange(side, dtype=jnp.int32)
    keep = (row_ids[:, None] < row_counts[block]) & (col_ids[None, :] < col_counts[block])
    grad_rows = jnp.where(keep, grads[0], jnp.zeros_like(grads[0]))
    left_rows = lax.dot_general(
        grad_rows,
        lax.all_gather(grad_rows, "tensor", axis=0, tiled=True),
        (((1,), (1,)), ((), ())),
        preferred_element_type=jnp.float32,
    )
    right_rows = lax.psum_scatter(
        lax.dot_general(
            grad_rows, grad_rows, (((0,), (0,)), ((), ())), preferred_element_type=jnp.float32
        ),
        "tensor",
        scatter_dimension=0,
        tiled=True,
    )
    left_stat = (left_rows / side).astype(jnp.bfloat16)
    right_stat = (right_rows / side).astype(jnp.bfloat16)
    stats = jnp.stack([left_stat, right_stat])
    olds = jnp.stack([old_left[0], old_right[0]])
    stat_list = [stats]
    old_list = [olds]
    for offset in range(1, TRAINERS):
        got_stats, got_olds = from_behind((stats, olds), "fsdp", -offset)
        stat_list.append(got_stats)
        old_list.append(got_olds)
    per_lane = 2 * TRAINERS // lanes
    stat_all = jnp.concatenate(stat_list, axis=0).reshape(lanes, per_lane, local_rows, side)
    old_all = jnp.concatenate(old_list, axis=0).reshape(lanes, per_lane, local_rows, side)
    owner_flag = block % TRAINERS == 0
    stat_items = lax.all_to_all(stat_all, "tensor", split_axis=0, concat_axis=2, tiled=True)
    old_items = lax.all_to_all(old_all, "tensor", split_axis=0, concat_axis=2, tiled=True)
    fresh = jax.vmap(refresh_one, in_axes=(0, 0, None))(stat_items[0], old_items[0], owner_flag)
    fresh_all = fresh[None]
    returned = lax.all_to_all(
        shortened(fresh_all), "tensor", split_axis=2, concat_axis=0, tiled=True
    ).astype(fresh_all.dtype)
    returned = returned.reshape(2 * TRAINERS, local_rows, side)
    result = returned[0:2]
    for offset in range(1, TRAINERS):
        got_bases = from_behind(shortened(returned[2 * offset : 2 * offset + 2]), "fsdp", offset)
        result = jnp.where(block % TRAINERS == offset, got_bases, result)
    return (result[0][None], result[1][None])


def solution(mesh):
    in_specs = (
        P("fsdp", "tensor", None),
        P(),
        P(),
        P("fsdp", "tensor", None),
        P("fsdp", "tensor", None),
    )
    out_specs = (P("fsdp", "tensor", None), P("fsdp", "tensor", None))
    return jax.shard_map(body, mesh=mesh, in_specs=in_specs, out_specs=out_specs, check_vma=False)
```

profile of v0, /device:TPU:6, one launch (start us, length us, event | category | flops | bytes accessed | tf_op | source)
XLA Modules:
  0.0 671.9 jit_solution(3951252733891016976)
XLA Ops:
  19.2 10.6 %collective-permute-start.3 = (bf16[2,128,1024]{2,1,0:T(8,128)(2,1)S(1)}, bf16[2,128,1024]{2,1,0:T(8,128)(2,1)S(1)}, u32[]{:S(2)}, u32[]{:S(2)}) collective-permute-start(bf16[2,128,1024]{2,1,0:T(8,128)(2,1)S(1)} %get-tuple-element.11), channel_id=1, source_target_pairs={{8,0},{16,8},{24,16},{32,24},{40,32},{48,40},{56,48},{64,56},{72,6... | collective-permute-start | bytes 1572872 | tf_op jit(solution)/shard_map/ppermute | solution.py:12
  40.9 16.0 %collective-permute-done.4 = bf16[2,128,1024]{2,1,0:T(8,128)(2,1)S(1)} collective-permute-done((bf16[2,128,1024]{2,1,0:T(8,128)(2,1)S(1)}, bf16[2,128,1024]{2,1,0:T(8,128)(2,1)S(1)}, u32[]{:S(2)}, u32[]{:S(2)}) %collective-permute-start.4) | collective-permute-done | bytes 524320 | tf_op jit(solution)/shard_map/ppermute | solution.py:12
  75.8 82.5 %reduce-scatter.2.cloned.1.call-done = f32[128,1024]{1,0:T(8,128)} async-done(((f32[1024,1024]{1,0:T(8,128)}), f32[128,1024]{1,0:T(8,128)}) %reduce-scatter.2.cloned.1.call-update) | async-done | bytes 524304 | tf_op jit(solution)/shard_map/reduce_scatter | solution.py:90
  173.4 13.5 %collective-permute-done.1 = bf16[2,128,1024]{2,1,0:T(8,128)(2,1)S(1)} collective-permute-done((bf16[2,128,1024]{2,1,0:T(8,128)(2,1)S(1)}, bf16[2,128,1024]{2,1,0:T(8,128)(2,1)S(1)}, u32[]{:S(2)}, u32[]{:S(2)}) %collective-permute-start.1) | collective-permute-done | bytes 524320 | tf_op jit(solution)/shard_map/ppermute | solution.py:12
  200.9 52.3 %all-to-all-done = bf16[8,1,128,1024]{3,2,1,0:T(8,128)(2,1)} async-done(((bf16[8,1,128,1024]{3,2,1,0:T(8,128)(2,1)}), bf16[8,1,128,1024]{3,2,1,0:T(8,128)(2,1)}, u32[]{:S(2)}, u32[]{:S(2)}) %all-to-all-start) | async-done | bytes 2097184 | tf_op jit(solution)/shard_map/all_to_all | solution.py:112
  262.5 11.7 %custom-call.48 = f32[1,128,128]{2,1,0:T(8,128)S(1)} custom-call(f32[1,128,128]{2,1,0:T(8,128)S(1)} %fusion.162), custom_call_target="Cholesky" | custom-call | tf_op jit(solution)/shard_map/vmap(jit(cholesky))/cholesky | solution.py:49
  275.6 9.8 %custom-call.49 = f32[1,1,128,128]{2,3,1,0:T(8,128)S(1)} custom-call(f32[1,1,128,128]{3,2,1,0:T(8,128)S(1)} %fusion.125), custom_call_target="InvertDiagBlocksLowerTriangular" | custom-call | tf_op jit(solution)/shard_map/vmap()/triangular_solve/custom-call.0 | solution.py:66
  289.1 12.2 %custom-call.50 = f32[1,128,128]{2,1,0:T(8,128)S(1)} custom-call(f32[1,128,128]{2,1,0:T(8,128)S(1)} %fusion.159), custom_call_target="Cholesky" | custom-call | tf_op jit(solution)/shard_map/vmap(jit(cholesky))/cholesky | solution.py:49
  302.7 9.8 %custom-call.51 = f32[1,1,128,128]{2,3,1,0:T(8,128)S(1)} custom-call(f32[1,1,128,128]{3,2,1,0:T(8,128)S(1)} %fusion.126), custom_call_target="InvertDiagBlocksLowerTriangular" | custom-call | tf_op jit(solution)/shard_map/vmap()/triangular_solve/custom-call.0 | solution.py:66
  317.9 11.9 %custom-call.52 = f32[1,128,128]{2,1,0:T(8,128)S(1)} custom-call(f32[1,128,128]{2,1,0:T(8,128)S(1)} %fusion.155), custom_call_target="Cholesky" | custom-call | tf_op jit(solution)/shard_map/vmap(jit(cholesky))/cholesky | solution.py:49
  331.1 9.8 %custom-call.53 = f32[1,1,128,128]{2,3,1,0:T(8,128)S(1)} custom-call(f32[1,1,128,128]{3,2,1,0:T(8,128)S(1)} %fusion.127), custom_call_target="InvertDiagBlocksLowerTriangular" | custom-call | tf_op jit(solution)/shard_map/vmap()/triangular_solve/custom-call.0 | solution.py:66
  345.7 11.7 %custom-call.54 = f32[1,128,128]{2,1,0:T(8,128)S(1)} custom-call(f32[1,128,128]{2,1,0:T(8,128)S(1)} %fusion.151), custom_call_target="Cholesky" | custom-call | tf_op jit(solution)/shard_map/vmap(jit(cholesky))/cholesky | solution.py:49
  358.7 9.8 %custom-call.55 = f32[1,1,128,128]{2,3,1,0:T(8,128)S(1)} custom-call(f32[1,1,128,128]{3,2,1,0:T(8,128)S(1)} %fusion.128), custom_call_target="InvertDiagBlocksLowerTriangular" | custom-call | tf_op jit(solution)/shard_map/vmap()/triangular_solve/custom-call.0 | solution.py:66
  373.5 11.7 %custom-call.56 = f32[1,128,128]{2,1,0:T(8,128)S(1)} custom-call(f32[1,128,128]{2,1,0:T(8,128)S(1)} %fusion.147), custom_call_target="Cholesky" | custom-call | tf_op jit(solution)/shard_map/vmap(jit(cholesky))/cholesky | solution.py:49
  386.5 9.8 %custom-call.57 = f32[1,1,128,128]{2,3,1,0:T(8,128)S(1)} custom-call(f32[1,1,128,128]{3,2,1,0:T(8,128)S(1)} %fusion.129), custom_call_target="InvertDiagBlocksLowerTriangular" | custom-call | tf_op jit(solution)/shard_map/vmap()/triangular_solve/custom-call.0 | solution.py:66
  400.5 12.1 %custom-call.58 = f32[1,128,128]{2,1,0:T(8,128)S(1)} custom-call(f32[1,128,128]{2,1,0:T(8,128)S(1)} %fusion.143), custom_call_target="Cholesky" | custom-call | tf_op jit(solution)/shard_map/vmap(jit(cholesky))/cholesky | solution.py:49
  413.9 9.8 %custom-call.59 = f32[1,1,128,128]{2,3,1,0:T(8,128)S(1)} custom-call(f32[1,1,128,128]{3,2,1,0:T(8,128)S(1)} %fusion.130), custom_call_target="InvertDiagBlocksLowerTriangular" | custom-call | tf_op jit(solution)/shard_map/vmap()/triangular_solve/custom-call.0 | solution.py:66
  468.8 11.7 %custom-call.60 = f32[1,128,128]{2,1,0:T(8,128)S(1)} custom-call(f32[1,128,128]{2,1,0:T(8,128)S(1)} %fusion.139), custom_call_target="Cholesky" | custom-call | tf_op jit(solution)/shard_map/vmap(jit(cholesky))/cholesky | solution.py:49
  481.8 10.1 %custom-call.61 = f32[1,1,128,128]{2,3,1,0:T(8,128)S(1)} custom-call(f32[1,1,128,128]{3,2,1,0:T(8,128)S(1)} %fusion.131), custom_call_target="InvertDiagBlocksLowerTriangular" | custom-call | tf_op jit(solution)/shard_map/vmap()/triangular_solve/custom-call.0 | solution.py:66
  493.8 11.7 %custom-call.62 = f32[1,128,128]{2,1,0:T(8,128)S(1)} custom-call(f32[1,128,128]{2,1,0:T(8,128)S(1)} %fusion.135), custom_call_target="Cholesky" | custom-call | tf_op jit(solution)/shard_map/vmap(jit(cholesky))/cholesky | solution.py:49
  525.2 10.8 %copy.125 = bf16[1,1,1024,1024]{3,1,0,2:T(2,128)(2,1)} copy(bf16[1,1,1024,1024]{2,3,1,0:T(8,128)(2,1)} %fusion.45) | data formatting | bytes 4194304 | tf_op jit(solution)/shard_map/vmap()/concatenate | solution.py:70
  536.6 12.8 %reduce.7 = bf16[1024,1024]{1,0:T(8,128)(2,1)S(1)} reduce(bf16[1024,1,1,1024]{3,2,1,0:T(2,128)(2,1)} %bitcast.789, bf16[]{:T(256)} %broadcast.203), dimensions={1,2}, to_apply=%bitcast.732.reduce_sub_computation | reduce | bytes 4194306
  553.1 55.3 %all_to_all.30 = bf16[8,2,65536]{2,1,0:T(2,128)(2,1)S(1)} all-to-all(bf16[8,2,65536]{2,1,0:T(2,128)(2,1)} %reshape.825), channel_id=1, replica_groups=mesh['fsdp'=64,'tensor'=8] {'tensor'}, dimensions={0} | all-to-all | bytes 4194304 | tf_op jit(solution)/shard_map/all_to_all | solution.py:116
  642.6 21.4 %collective-permute-done.6 = bf16[2,128,1024]{2,1,0:T(8,128)(2,1)} collective-permute-done((bf16[2,128,1024]{2,1,0:T(8,128)(2,1)S(1)}, bf16[2,128,1024]{2,1,0:T(8,128)(2,1)}, u32[]{:S(2)}, u32[]{:S(2)}) %collective-permute-start.6) | collective-permute-done | bytes 524320 | tf_op jit(solution)/shard_map/ppermute | solution.py:12
  (229 shorter events, 217.5 us)
Async XLA Ops:
  7.2 65.5 %all-gather.2.cloned.1.call-start = ((), (), s32[]{:S(2)}) async-start(), calls=%async_computation.4 | async-start | bytes 2359296 | tf_op jit(solution)/shard_map/all_gather | solution.py:86
  12.8 145.4 %reduce-scatter.2.cloned.1.call-start = ((), (), s32[]{:S(2)}) async-start(), calls=%async_computation.5 | async-start | bytes 4718592 | tf_op jit(solution)/shard_map/reduce_scatter | solution.py:90
  19.2 20.9 %collective-permute-start.3 = (bf16[2,128,1024]{2,1,0:T(8,128)(2,1)S(1)}, bf16[2,128,1024]{2,1,0:T(8,128)(2,1)S(1)}, u32[]{:S(2)}, u32[]{:S(2)}) collective-permute-start(bf16[2,128,1024]{2,1,0:T(8,128)(2,1)S(1)} %get-tuple-element.11), channel_id=1, source_target_pairs={{8,0},{16,8},{24,16},{32,24},{40,32},{48,40},{56,48},{64,56},{72,6... | collective-permute-start | bytes 1572872 | tf_op jit(solution)/shard_map/ppermute | solution.py:12
  29.8 27.1 %collective-permute-start.4 = (bf16[2,128,1024]{2,1,0:T(8,128)(2,1)S(1)}, bf16[2,128,1024]{2,1,0:T(8,128)(2,1)S(1)}, u32[]{:S(2)}, u32[]{:S(2)}) collective-permute-start(bf16[2,128,1024]{2,1,0:T(8,128)(2,1)S(1)} %get-tuple-element.11), channel_id=1, source_target_pairs={{16,0},{24,8},{32,16},{40,24},{48,32},{56,40},{64,48},{72,56},{80,... | collective-permute-start | bytes 1572872 | tf_op jit(solution)/shard_map/ppermute | solution.py:12
  32.3 32.3 %collective-permute-start.5 = (bf16[2,128,1024]{2,1,0:T(8,128)(2,1)S(1)}, bf16[2,128,1024]{2,1,0:T(8,128)(2,1)S(1)}, u32[]{:S(2)}, u32[]{:S(2)}) collective-permute-start(bf16[2,128,1024]{2,1,0:T(8,128)(2,1)S(1)} %get-tuple-element.11), channel_id=1, source_target_pairs={{24,0},{32,8},{40,16},{48,24},{56,32},{64,40},{72,48},{80,56},{88,... | collective-permute-start | bytes 1572872 | tf_op jit(solution)/shard_map/ppermute | solution.py:12
  65.4 7.3 %copy-start.1 = (bf16[128,1024]{1,0:T(8,128)(2,1)S(1)}, bf16[128,1024]{1,0:T(8,128)(2,1)}, u32[]{:S(2)}) copy-start(bf16[128,1024]{1,0:T(8,128)(2,1)} %and_select_fusion.1) | copy-start | bytes 786436
  65.4 130.0 %all-to-all-start.1 = ((bf16[8,1,128,1024]{3,2,1,0:T(8,128)(2,1)}), bf16[8,1,128,1024]{3,2,1,0:T(8,128)(2,1)S(1)}, u32[]{:S(2)}, u32[]{:S(2)}) async-start(bf16[8,1,128,1024]{3,2,1,0:T(8,128)(2,1)} %bitcast.9), calls=%async_computation.2 | async-start | bytes 4194304 | tf_op jit(solution)/shard_map/all_to_all | solution.py:113
  160.1 12.4 %collective-permute-start = (bf16[2,128,1024]{2,1,0:T(8,128)(2,1)S(1)}, bf16[2,128,1024]{2,1,0:T(8,128)(2,1)S(1)}, u32[]{:S(2)}, u32[]{:S(2)}) collective-permute-start(bf16[2,128,1024]{2,1,0:T(8,128)(2,1)S(1)} %pad_maximum_fusion), channel_id=1, source_target_pairs={{8,0},{16,8},{24,16},{32,24},{40,32},{48,40},{56,48},{64,56},{72,6... | collective-permute-start | bytes 1572872 | tf_op jit(solution)/shard_map/ppermute | solution.py:12
  162.1 24.9 %collective-permute-start.1 = (bf16[2,128,1024]{2,1,0:T(8,128)(2,1)S(1)}, bf16[2,128,1024]{2,1,0:T(8,128)(2,1)S(1)}, u32[]{:S(2)}, u32[]{:S(2)}) collective-permute-start(bf16[2,128,1024]{2,1,0:T(8,128)(2,1)S(1)} %pad_maximum_fusion), channel_id=1, source_target_pairs={{16,0},{24,8},{32,16},{40,24},{48,32},{56,40},{64,48},{72,56},{80,... | collective-permute-start | bytes 1572872 | tf_op jit(solution)/shard_map/ppermute | solution.py:12
  169.5 25.0 %collective-permute-start.2 = (bf16[2,128,1024]{2,1,0:T(8,128)(2,1)S(1)}, bf16[2,128,1024]{2,1,0:T(8,128)(2,1)S(1)}, u32[]{:S(2)}, u32[]{:S(2)}) collective-permute-start(bf16[2,128,1024]{2,1,0:T(8,128)(2,1)S(1)} %pad_maximum_fusion), channel_id=1, source_target_pairs={{24,0},{32,8},{40,16},{48,24},{56,32},{64,40},{72,48},{80,56},{88,... | collective-permute-start | bytes 1572872 | tf_op jit(solution)/shard_map/ppermute | solution.py:12
  195.4 57.8 %all-to-all-start = ((bf16[8,1,128,1024]{3,2,1,0:T(8,128)(2,1)}), bf16[8,1,128,1024]{3,2,1,0:T(8,128)(2,1)}, u32[]{:S(2)}, u32[]{:S(2)}) async-start(bf16[8,1,128,1024]{3,2,1,0:T(8,128)(2,1)} %bitcast.7), calls=%async_computation.1 | async-start | bytes 4194304 | tf_op jit(solution)/shard_map/all_to_all | solution.py:112
  396.3 29.0 %copy-start.18 = (f32[1,1,128,128]{2,3,1,0:T(8,128)S(1)}, f32[1,1,128,128]{2,3,1,0:T(8,128)}, u32[]{:S(2)}) copy-start(f32[1,1,128,128]{2,3,1,0:T(8,128)} %copy-done.17) | copy-start | bytes 196612
  400.4 29.2 %copy-start.26 = (f32[1,1,128,128]{2,3,1,0:T(8,128)S(1)}, f32[1,1,128,128]{2,3,1,0:T(8,128)}, u32[]{:S(2)}) copy-start(f32[1,1,128,128]{2,3,1,0:T(8,128)} %copy-done.25) | copy-start | bytes 196612
  432.9 4.9 copy-start.7
  462.4 5.0 copy-start.9
  462.4 5.0 copy-start.10
  463.8 28.8 %copy-start.13 = (f32[1,128,128]{1,2,0:T(8,128)S(1)}, f32[1,128,128]{1,2,0:T(8,128)}, u32[]{:S(2)}) copy-start(f32[1,128,128]{1,2,0:T(8,128)} %convolution_bitcast_fusion.55) | copy-start | bytes 196612
  463.8 28.8 %copy-start.14 = (f32[1,128,128]{1,2,0:T(8,128)S(1)}, f32[1,128,128]{1,2,0:T(8,128)}, u32[]{:S(2)}) copy-start(f32[1,128,128]{1,2,0:T(8,128)} %convolution_bitcast_fusion.54) | copy-start | bytes 196612
  463.8 28.8 %copy-start.15 = (f32[1,128,128]{1,2,0:T(8,128)S(1)}, f32[1,128,128]{1,2,0:T(8,128)}, u32[]{:S(2)}) copy-start(f32[1,128,128]{1,2,0:T(8,128)} %convolution_bitcast_fusion.53) | copy-start | bytes 196612
  463.8 28.8 %copy-start.16 = (f32[1,128,128]{1,2,0:T(8,128)S(1)}, f32[1,128,128]{1,2,0:T(8,128)}, u32[]{:S(2)}) copy-start(f32[1,128,128]{1,2,0:T(8,128)} %convolution_bitcast_fusion.52) | copy-start | bytes 196612
  467.4 49.3 %copy-start.2 = (f32[1,1024,128]{2,1,0:T(8,128)S(1)}, f32[1,1024,128]{2,1,0:T(8,128)}, u32[]{:S(2)}) copy-start(f32[1,1024,128]{2,1,0:T(8,128)} %convolution_bitcast_fusion.12) | copy-start | bytes 1572868
  619.9 17.0 %collective-permute-start.8 = (bf16[2,128,1024]{2,1,0:T(8,128)(2,1)S(1)}, bf16[2,128,1024]{2,1,0:T(8,128)(2,1)S(1)}, u32[]{:S(2)}, u32[]{:S(2)}) collective-permute-start(bf16[2,128,1024]{2,1,0:T(8,128)(2,1)S(1)} %bitcast.842), channel_id=1, source_target_pairs={{0,8},{8,16},{16,24},{24,32},{32,40},{40,48},{48,56},{56,64},{64,7... | collective-permute-start | bytes 1572872 | tf_op jit(solution)/shard_map/ppermute | solution.py:12
  621.8 20.8 %collective-permute-start.7 = (bf16[2,128,1024]{2,1,0:T(8,128)(2,1)S(1)}, bf16[2,128,1024]{2,1,0:T(8,128)(2,1)}, u32[]{:S(2)}, u32[]{:S(2)}) collective-permute-start(bf16[2,128,1024]{2,1,0:T(8,128)(2,1)S(1)} %bitcast.841), channel_id=1, source_target_pairs={{0,16},{8,24},{16,32},{24,40},{32,48},{40,56},{48,64},{56,72},{64,... | collective-permute-start | bytes 1572872 | tf_op jit(solution)/shard_map/ppermute | solution.py:12
  623.8 40.1 %collective-permute-start.6 = (bf16[2,128,1024]{2,1,0:T(8,128)(2,1)S(1)}, bf16[2,128,1024]{2,1,0:T(8,128)(2,1)}, u32[]{:S(2)}, u32[]{:S(2)}) collective-permute-start(bf16[2,128,1024]{2,1,0:T(8,128)(2,1)S(1)} %slice_bitcast_fusion), channel_id=1, source_target_pairs={{0,24},{8,32},{16,40},{24,48},{32,56},{40,64},{48,72},{56,80},{64,... | collective-permute-start | bytes 1572872 | tf_op jit(solution)/shard_map/ppermute | solution.py:12
  (18 other events, 46.0 us)
Sparse Core Ops, SparseCore 0:
  13.0 48.3 all-gather.1
  64.2 94.0 reduce-scatter.1
where the time goes:
time: 676 us; the launch traced here: 672 us
  waiting for transfers between devices  221 us (33%)
  other arithmetic  203 us (30%)
  matrix products  90 us (13%)
  blocking collectives  55.3 us (8%)
  starting transfers between devices  47.4 us (7%)
  local copies, waits for them, and re-layouts  40.2 us (6%)
  between operations  15.5 us (2%)
    another operation x24, other arithmetic, refresh_one(): diag_block = jnp.linalg.cholesky(column[:width])  100 us
    ppermute x9, waiting for transfers between devices, from_behind(): return lax.ppermute(block, axis, route)  85.7 us
    another operation x16, other arithmetic, refresh_one(): lax.linalg.triangular_solve(diag_block, rhs, left_side=False, lower=True,...  84 us
    reduce_scatter x1, waiting for transfers between devices, body(): lax.psum_scatter(lax.dot_general(grad_rows, grad_rows, (((0,), (0,)), (()...  82.5 us
    dot_general x56, matrix products, product_nt(): lax.dot_general(left, right, (((1,), (1,)), ((), ())), precision=lax.Prec...  59.4 us
    all_to_all x1, blocking collectives, body(): lax.all_to_all(shortened(fresh_all), 'tensor', split_axis=2, concat_axis=...  55.3 us
    all_to_all x1, waiting for transfers between devices, body(): lax.all_to_all(stat_all, 'tensor', split_axis=0, concat_axis=2, tiled=True)  52.3 us
    ppermute x9, starting transfers between devices, from_behind(): return lax.ppermute(block, axis, route)  34.6 us
  transfers between devices with their start and end apart: 13, of which 11 were waited for; matrix products, arithmetic and copies ran while one was open for 2% of the time, Pallas kernels for 0%

commit v1 on v0

v1 whole, which is shorter than its diff:
```python
import functools

import jax
import jax.numpy as jnp
from jax import lax
from jax.experimental import pallas as pl
from jax.experimental.pallas import tpu as pltpu
from jax.sharding import PartitionSpec as P

MESH = pl.DeviceIdType.MESH
BF16 = jnp.bfloat16
F32 = jnp.float32
NB = 128
VMEM_LIMIT = 56 * 1024 * 1024


def workers(lanes):
    core = lax.rem(lax.axis_index("fsdp"), 2)
    left = core * (lanes // 4)
    return left, left + lanes // 2


def ring_barrier(lanes, me):
    barrier = pltpu.get_barrier_semaphore()
    for step in range(1, lanes):
        other = lax.rem(me + step, lanes)
        pl.semaphore_signal(barrier, inc=1, device_id={"tensor": other}, device_id_type=MESH)
    pl.semaphore_wait(barrier, lanes - 1)


def gather_kernel(lanes, rc_ref, cc_ref, g_ref, l_ref, r_ref, gout, pout, gm, ssem, gsem, psem, osem):
    me = lax.axis_index("tensor")
    block = lax.axis_index("fsdp")
    rows, side = g_ref.shape
    left, right = workers(lanes)
    rid = me * rows + lax.broadcasted_iota(jnp.int32, (rows, side), 0)
    cid = lax.broadcasted_iota(jnp.int32, (rows, side), 1)
    keep = (rid < rc_ref[block]) & (cid < cc_ref[block])
    gm[...] = jnp.where(keep, g_ref[...].astype(F32), 0.0).astype(BF16)
    ring_barrier(lanes, me)
    mine = pl.ds(pl.multiple_of(me * rows, rows), rows)

    def remote(src, dst, k, sem, to):
        return pltpu.make_async_remote_copy(
            src_ref=src, dst_ref=dst.at[mine], send_sem=ssem.at[k], recv_sem=sem.at[me],
            device_id={"tensor": to}, device_id_type=MESH,
        )

    jobs = []
    for k, (src, dst, sem, to) in enumerate(
        ((gm, gout, gsem, left), (gm, gout, gsem, right), (l_ref, pout, psem, left), (r_ref, pout, psem, right))
    ):
        jobs.append((to, src, dst, k, remote(src, dst, k, sem, to)))
    for to, src, dst, k, copy in jobs:
        @pl.when(me != to)
        def _():
            copy.start()

        @pl.when(me == to)
        def _():
            pltpu.make_async_copy(src, dst.at[mine], osem.at[k]).start()
    for to, src, dst, k, copy in jobs:
        @pl.when(me != to)
        def _():
            copy.wait_send()

        @pl.when(me == to)
        def _():
            pltpu.make_async_copy(src, dst.at[mine], osem.at[k]).wait()

    @pl.when((me == left) | (me == right))
    def _():
        for step in range(1, lanes):
            other = lax.rem(me + step, lanes)
            theirs = pl.ds(pl.multiple_of(other * rows, rows), rows)
            for src, dst, sem in ((gm, gout, gsem), (l_ref, pout, psem)):
                pltpu.make_async_remote_copy(
                    src_ref=src, dst_ref=dst.at[theirs], send_sem=ssem.at[0], recv_sem=sem.at[other],
                    device_id={"tensor": other}, device_id_type=MESH,
                ).wait_recv()


def scatter_kernel(lanes, x_ref, lout, rout, ssem, rsem, osem):
    me = lax.axis_index("tensor")
    rows = lout.shape[0]
    left, right = workers(lanes)
    ring_barrier(lanes, me)

    def copy_to(which, out, step):
        other = lax.rem(me + step, lanes)
        theirs = pl.ds(pl.multiple_of(other * rows, rows), rows)
        return pltpu.make_async_remote_copy(
            src_ref=x_ref.at[theirs], dst_ref=out, send_sem=ssem.at[step], recv_sem=rsem.at[which],
            device_id={"tensor": other}, device_id_type=MESH,
        )

    mine = pl.ds(pl.multiple_of(me * rows, rows), rows)
    for which, (worker, out) in enumerate(((left, lout), (right, rout))):
        @pl.when(me == worker)
        def _():
            for step in range(1, lanes):
                copy_to(which, out, step).start()
            pltpu.make_async_copy(x_ref.at[mine], out, osem).start()
            for step in range(1, lanes):
                copy_to(which, out, step).wait_send()
            pltpu.make_async_copy(x_ref.at[mine], out, osem).wait()

    for which, (worker, out) in enumerate(((left, lout), (right, rout))):
        @pl.when(me != worker)
        def _():
            copy_to(which, out, 1).wait_recv()


def across(column):
    return jnp.broadcast_to(column, (8, NB))


def inverse_rcp(x):
    r = pl.reciprocal(x, approx=True)
    return r * (2.0 - x * r)


def diag_inverse(load):
    count = NB // 8
    sub = lax.broadcasted_iota(jnp.int32, (8, NB), 0)
    lane = lax.broadcasted_iota(jnp.int32, (8, NB), 1)
    rows = [load(i) for i in range(count)]
    done = []
    for r in range(count):
        k0 = 8 * r
        inside = (lane >= k0) & (lane < k0 + 8)
        top = rows[r]
        cols = [across(top[:, k0 + q : k0 + q + 1]) for q in range(8)]
        top = jnp.where(lane - k0 == sub, 1.0, jnp.where(inside, 0.0, top))
        rcp, upper, flat = [], [], []
        scale = jnp.zeros((8, NB), F32)
        for p in range(8):
            pivot = across(cols[p][p : p + 1, :])
            inv = inverse_rcp(pivot)
            scale = jnp.where(sub == p, lax.rsqrt(pivot), scale)
            mult = jnp.where(sub > p, cols[p] * inv, 0.0)
            line = {}
            for q in range(p + 1, 8):
                line[q] = across(cols[q][p : p + 1, :])
                cols[q] = cols[q] - mult * line[q]
            row = across(top[p : p + 1, :])
            top = top - mult * row
            rcp.append(inv)
            upper.append(line)
            flat.append(row)
        done.append(jnp.where(lane <= sub + k0, top * scale, 0.0))
        for i in range(r + 1, count):
            body = rows[i]
            cols = [across(body[:, k0 + q : k0 + q + 1]) for q in range(8)]
            body = jnp.where(inside, 0.0, body)
            for p in range(8):
                w = cols[p] * rcp[p]
                for q in range(p + 1, 8):
                    cols[q] = cols[q] - w * upper[p][q]
                body = body - w * flat[p]
            rows[i] = body
    return done


def halves(x):
    high = x.astype(BF16)
    return high, (x - high.astype(F32)).astype(BF16)


def nt(a, b):
    return lax.dot_general(a, b, (((1,), (1,)), ((), ())), preferred_element_type=F32)


def nn(a, b):
    return jnp.dot(a, b, preferred_element_type=F32)


def tn(a, b):
    return lax.dot_general(a, b, (((0,), (0,)), ((), ())), preferred_element_type=F32)


def refresh_kernel(role_ref, g_ref, p_ref, x_ref, s_ref, w_ref, a_ref, nh, nl, lcat, rcat, m_ref):
    side = g_ref.shape[0]
    tile = min(256, side)
    tiles = side // tile
    role = role_ref[0]

    def at(t):
        return pl.ds(pl.multiple_of(t * tile, tile), tile)

    @pl.when(role == 0)
    def _():
        @pl.loop(0, tiles)
        def _(t):
            s_ref[at(t), :] = (nt(g_ref[at(t), :], g_ref[...]) * (1.0 / side)).astype(BF16)

    @pl.when(role == 1)
    def _():
        @pl.loop(0, tiles)
        def _(t):
            s_ref[at(t), :] = (tn(g_ref[:, at(t)], g_ref[...]) * (1.0 / side)).astype(BF16)

    @pl.when(role < 2)
    def _():
        @pl.loop(0, tiles)
        def _(t):
            w_ref[at(t), :] = (nn(s_ref[at(t), :], p_ref[...]) + p_ref[at(t), :].astype(F32)).astype(BF16)

        @pl.loop(0, tiles)
        def _(t):
            a_ref[at(t), :] = tn(w_ref[:, at(t)], w_ref[...])

        @pl.loop(0, side // NB)
        def _(j):
            start = pl.multiple_of(j * NB, NB)
            here = pl.ds(start, NB)
            done = diag_inverse(lambda i: a_ref[pl.ds(start + 8 * i, 8), here])
            for i, part in enumerate(done):
                m_ref[8 * i : 8 * i + 8, :] = part
            inv = m_ref[...]
            mh, ml = halves(inv)
            rid = lax.broadcasted_iota(jnp.int32, (side, NB), 0)
            column = a_ref[:, here]
            below = rid >= start + NB
            ch, cl = halves(jnp.where(below, column, 0.0))
            low = nt(ch, mh) + nt(cl, mh) + nt(ch, ml)
            lh, ll = halves(low)
            lcat[:, 0:NB] = lh
            lcat[:, NB : 2 * NB] = ll
            lcat[:, 2 * NB : 3 * NB] = lh
            a_ref[:, here] = jnp.where(below, 0.0, column)
            bh, bl = halves(a_ref[here, :])
            rcat[0:NB, :] = bh
            rcat[NB : 2 * NB, :] = bh
            rcat[2 * NB : 3 * NB, :] = bl
            fresh = nn(jnp.concatenate([mh, ml, mh], axis=1), rcat[...])
            a_ref[here, :] = fresh
            a_ref[here, here] = inv
            fh, fl = halves(a_ref[here, :])
            rcat[0:NB, :] = fh
            rcat[NB : 2 * NB, :] = fh
            rcat[2 * NB : 3 * NB, :] = fl
            cid = lax.broadcasted_iota(jnp.int32, (NB, side), 1)
            kept = cid < start + NB
            nh[here, :] = jnp.where(kept, fh.astype(F32), 0.0).astype(BF16)
            nl[here, :] = jnp.where(kept, fl.astype(F32), 0.0).astype(BF16)

            @pl.loop((j + 1) * NB // tile, tiles)
            def _(t):
                a_ref[at(t), :] = a_ref[at(t), :] - nn(lcat[at(t), :], rcat[...])

        @pl.loop(0, tiles)
        def _(t):
            x_ref[at(t), :] = (nt(w_ref[at(t), :], nh[...]) + nt(w_ref[at(t), :], nl[...])).astype(BF16)


def refresh_call(role, grad, basis):
    side = grad.shape[0]
    vmem = pl.BlockSpec(memory_space=pltpu.VMEM)
    return pl.pallas_call(
        refresh_kernel,
        out_shape=jax.ShapeDtypeStruct((side, side), BF16),
        in_specs=[pl.BlockSpec(memory_space=pltpu.SMEM), vmem, vmem],
        out_specs=vmem,
        scratch_shapes=[
            pltpu.VMEM((side, side), BF16),
            pltpu.VMEM((side, side), BF16),
            pltpu.VMEM((side, side), F32),
            pltpu.VMEM((side, side), BF16),
            pltpu.VMEM((side, side), BF16),
            pltpu.VMEM((side, 3 * NB), BF16),
            pltpu.VMEM((3 * NB, side), BF16),
            pltpu.VMEM((NB, NB), F32),
        ],
        compiler_params=pltpu.CompilerParams(vmem_limit_bytes=VMEM_LIMIT),
        cost_estimate=pl.CostEstimate(flops=14 * side**3, bytes_accessed=6 * side * side, transcendentals=0),
        name="refresh",
    )(role, grad, basis)


def body(grads, row_counts, col_counts, old_left, old_right):
    rows, side = grads.shape[1:]
    lanes = lax.axis_size("tensor")
    me = lax.axis_index("tensor")
    vmem = pl.BlockSpec(memory_space=pltpu.VMEM)
    smem = pl.BlockSpec(memory_space=pltpu.SMEM)
    hbm = pl.BlockSpec(memory_space=pl.ANY)
    whole = jax.ShapeDtypeStruct((side, side), BF16)
    part = jax.ShapeDtypeStruct((rows, side), BF16)
    dma = pltpu.SemaphoreType.DMA
    grad, basis = pl.pallas_call(
        functools.partial(gather_kernel, lanes),
        out_shape=(whole, whole),
        in_specs=[smem, smem, vmem, vmem, vmem],
        out_specs=(hbm, hbm),
        scratch_shapes=[pltpu.VMEM((rows, side), BF16), dma((4,)), dma((lanes,)), dma((lanes,)), dma((4,))],
        compiler_params=pltpu.CompilerParams(
            collective_id=0, has_side_effects=True, vmem_limit_bytes=VMEM_LIMIT
        ),
        name="gather",
    )(row_counts, col_counts, grads[0], old_left[0], old_right[0])
    left, right = workers(lanes)
    role = jnp.where(me == left, 0, jnp.where(me == right, 1, 2)).astype(jnp.int32).reshape(1)
    fresh = refresh_call(role, grad, basis)
    new_left, new_right = pl.pallas_call(
        functools.partial(scatter_kernel, lanes),
        out_shape=(part, part),
        in_specs=[hbm],
        out_specs=(hbm, hbm),
        scratch_shapes=[dma((lanes,)), dma((2,)), dma],
        compiler_params=pltpu.CompilerParams(
            collective_id=1, has_side_effects=True, vmem_limit_bytes=VMEM_LIMIT
        ),
        name="scatter",
    )(fresh)
    return (new_left[None], new_right[None])


def solution(mesh):
    split = P("fsdp", "tensor", None)
    return jax.shard_map(
        body, mesh=mesh, in_specs=(split, P(), P(), split, split), out_specs=(split, split), check_vma=False
    )
```

time: 676 us -> 141 us (0.21)
  waiting for transfers between devices: 221 us -> 0 us
  other arithmetic: 203 us -> 0 us
  Pallas kernels: 0 us -> 137 us
  matrix products: 90 us -> 0 us
  blocking collectives: 55.3 us -> 0 us
  starting transfers between devices: 47.4 us -> 0 us
  local copies, waits for them, and re-layouts: 40.2 us -> 3.34 us
  between operations: 15.5 us -> 0.66 us
    another operation x41 -> x0, other arithmetic: 184 us -> none  [the longest x24 100 us: refresh_one(): diag_block = jnp.linalg.cholesky(column[:width])]
    pallas_call x0 -> x3, Pallas kernels: none -> 137 us  [the longest x1 68.8 us: refresh_call(): pl.pallas_call(refresh_kernel, out_shape=jax.ShapeDtypeStruct((side, side...]
    ppermute x9 -> x0, waiting for transfers between devices: 85.7 us -> none  [from_behind(): return lax.ppermute(block, axis, route)]
    reduce_scatter x1 -> x0, waiting for transfers between devices: 82.5 us -> none  [body(): lax.psum_scatter(lax.dot_general(grad_rows, grad_rows, (((0,), (0,)), (()...]
    dot_general x60 -> x0, matrix products: 72.6 us -> none  [the longest x56 59.4 us: product_nt(): lax.dot_general(left, right, (((1,), (1,)), ((), ())), precision=lax.Prec...]
    all_to_all x1 -> x0, blocking collectives: 55.3 us -> none  [body(): lax.all_to_all(shortened(fresh_all), 'tensor', split_axis=2, concat_axis=...]
    all_to_all x2 -> x0, waiting for transfers between devices: 52.3 us -> none  [the longest x1 52.3 us: body(): lax.all_to_all(stat_all, 'tensor', split_axis=0, concat_axis=2, tiled=True)]
    ppermute x9 -> x0, starting transfers between devices: 34.6 us -> none  [from_behind(): return lax.ppermute(block, axis, route)]
  transfers between devices with their start and end apart: 13 -> 0, of which waited for: 11 -> 0; matrix products, arithmetic and copies ran while one was open for 2% -> 0% of each run, Pallas kernels for 0% -> 0%
where the time goes in v1:
time: 141 us
  Pallas kernels  137 us (97%)
  local copies, waits for them, and re-layouts  3.34 us (2%)
    pallas_call x1, Pallas kernels, refresh_call(): pl.pallas_call(refresh_kernel, out_shape=jax.ShapeDtypeStruct((side, side...  68.8 us
    pallas_call x1, Pallas kernels, body(): pl.pallas_call(functools.partial(gather_kernel, lanes), out_shape=(whole,...  42.7 us
    pallas_call x1, Pallas kernels, body(): pl.pallas_call(functools.partial(scatter_kernel, lanes), out_shape=(part,...  25.5 us
    unnamed x2, local copies, waits for them, and re-layouts  3.34 us

profile of v1, /device:TPU:6, one launch (start us, length us, event | category | flops | bytes accessed | tf_op | source)
XLA Modules:
  0.0 141.0 jit_solution(8928439173554354185)
XLA Ops:
  0.6 42.7 %gather.1 = (bf16[1024,1024]{1,0:T(8,128)(2,1)}, bf16[1024,1024]{1,0:T(8,128)(2,1)}) custom-call(s32[64]{0:T(128)} %rc_ref.1, s32[64]{0:T(128)} %cc_ref.1, bf16[128,1024]{1,0:T(8,128)(2,1)} %bitcast.6, bf16[128,1024]{1,0:T(8,128)(2,1)} %bitcast.7, bf16[128,1024]{1,0:T(8,128)(2,1)} %bitcast.8), custom_call_target="tpu_custom_call" | custom-call | tf_op jit(solution)/shard_map/gather/pallas_call | solution.py:291
  43.4 68.8 %refresh.1.x_ref = bf16[1024,1024]{1,0:T(8,128)(2,1)} custom-call(s32[1]{0:T(128)} %bitcast.role_ref, bf16[1024,1024]{1,0:T(8,128)(2,1)} %get-tuple-element.6.g_ref, bf16[1024,1024]{1,0:T(8,128)(2,1)} %get-tuple-element.7.p_ref), custom_call_target="tpu_custom_call" | custom-call | flops 15032385536 | bytes 6291456 | tf_op jit(solution)/shard_map/refresh/pallas_call | solution.py:260
  112.2 25.5 %scatter.1 = (bf16[128,1024]{1,0:T(8,128)(2,1)}, bf16[128,1024]{1,0:T(8,128)(2,1)}) custom-call(bf16[1024,1024]{1,0:T(8,128)(2,1)} %refresh.1.x_ref), custom_call_target="tpu_custom_call" | custom-call | tf_op jit(solution)/shard_map/scatter/pallas_call | solution.py:305
  137.7 1.7 %copy.9 = bf16[1,128,1024]{2,1,0:T(8,128)(2,1)} copy(bf16[1,128,1024]{2,1,0:T(8,128)(2,1)} %bitcast.10) | data formatting | bytes 524288
  139.3 1.7 %copy.10 = bf16[1,128,1024]{2,1,0:T(8,128)(2,1)} copy(bf16[1,128,1024]{2,1,0:T(8,128)(2,1)} %bitcast.9) | data formatting | bytes 524288

commit v2 on v1

v2 whole, which is shorter than its diff:
```python
import functools

import jax
import jax.numpy as jnp
from jax import lax
from jax.experimental import pallas as pl
from jax.experimental.pallas import tpu as pltpu
from jax.sharding import PartitionSpec as P

MESH = pl.DeviceIdType.MESH
BF16 = jnp.bfloat16
F32 = jnp.float32
NB = 128
VMEM_LIMIT = 56 * 1024 * 1024


def workers(lanes):
    core = lax.rem(lax.axis_index("fsdp"), 2)
    left = core * (lanes // 4)
    return left, left + lanes // 2


def ring_barrier(lanes, me):
    barrier = pltpu.get_barrier_semaphore()
    for step in range(1, lanes):
        other = lax.rem(me + step, lanes)
        pl.semaphore_signal(barrier, inc=1, device_id={"tensor": other}, device_id_type=MESH)
    pl.semaphore_wait(barrier, lanes - 1)


def across(column):
    return jnp.broadcast_to(column, (8, NB))


def inverse_rcp(x):
    r = pl.reciprocal(x, approx=True)
    return r * (2.0 - x * r)


def diag_inverse(load):
    count = NB // 8
    sub = lax.broadcasted_iota(jnp.int32, (8, NB), 0)
    lane = lax.broadcasted_iota(jnp.int32, (8, NB), 1)
    rows = [load(i) for i in range(count)]
    done = []
    for r in range(count):
        k0 = 8 * r
        inside = (lane >= k0) & (lane < k0 + 8)
        top = rows[r]
        cols = [across(top[:, k0 + q : k0 + q + 1]) for q in range(8)]
        top = jnp.where(lane - k0 == sub, 1.0, jnp.where(inside, 0.0, top))
        rcp, upper, flat = [], [], []
        scale = jnp.zeros((8, NB), F32)
        for p in range(8):
            pivot = across(cols[p][p : p + 1, :])
            inv = inverse_rcp(pivot)
            scale = jnp.where(sub == p, lax.rsqrt(pivot), scale)
            mult = jnp.where(sub > p, cols[p] * inv, 0.0)
            line = {}
            for q in range(p + 1, 8):
                line[q] = across(cols[q][p : p + 1, :])
                cols[q] = cols[q] - mult * line[q]
            row = across(top[p : p + 1, :])
            top = top - mult * row
            rcp.append(inv)
            upper.append(line)
            flat.append(row)
        done.append(jnp.where(lane <= sub + k0, top * scale, 0.0))
        for i in range(r + 1, count):
            body = rows[i]
            cols = [across(body[:, k0 + q : k0 + q + 1]) for q in range(8)]
            body = jnp.where(inside, 0.0, body)
            for p in range(8):
                w = cols[p] * rcp[p]
                for q in range(p + 1, 8):
                    cols[q] = cols[q] - w * upper[p][q]
                body = body - w * flat[p]
            rows[i] = body
    return done


def halves(x):
    high = x.astype(BF16)
    return high, (x - high.astype(F32)).astype(BF16)


def nt(a, b):
    return lax.dot_general(a, b, (((1,), (1,)), ((), ())), preferred_element_type=F32)


def nn(a, b):
    return jnp.dot(a, b, preferred_element_type=F32)


def tn(a, b):
    return lax.dot_general(a, b, (((0,), (0,)), ((), ())), preferred_element_type=F32)


def eliminate(step, a_ref, m_ref, lcat, rcat, pair):
    side = a_ref.shape[0]
    start = pl.multiple_of(step * NB, NB)
    here = pl.ds(start, NB)
    mh, ml = halves(m_ref[...])
    scale_row(step, a_ref, m_ref, mh, ml, rcat, pair)
    below = lax.broadcasted_iota(jnp.int32, (side, NB), 0) >= start + NB
    column = a_ref[:, here]
    ch, cl = halves(jnp.where(below, column, 0.0))
    low = nt(jnp.concatenate([ch, cl, ch], axis=1), jnp.concatenate([mh, mh, ml], axis=1))
    lh, ll = halves(low)
    lcat[:, 0:NB] = lh
    lcat[:, NB : 2 * NB] = ll
    lcat[:, 2 * NB : 3 * NB] = lh
    a_ref[:, here] = jnp.where(below, 0.0, column)
    tile = min(256, side)
    for t in range(side // tile):
        cols = slice(t * tile, (t + 1) * tile)
        a_ref[:, cols] = a_ref[:, cols] - nn(lcat[...], rcat[:, cols])


def scale_row(step, a_ref, m_ref, mh, ml, rcat, pair):
    side = a_ref.shape[0]
    start = pl.multiple_of(step * NB, NB)
    here = pl.ds(start, NB)
    bh, bl = halves(a_ref[here, :])
    fresh = nn(
        jnp.concatenate([mh, ml, mh], axis=1), jnp.concatenate([bh, bh, bl], axis=0)
    )
    a_ref[here, :] = fresh
    a_ref[here, here] = m_ref[...]
    fresh = a_ref[here, :]
    fh, fl = halves(fresh)
    rcat[0:NB, :] = fh
    rcat[NB : 2 * NB, :] = fh
    rcat[2 * NB : 3 * NB, :] = fl
    kept = lax.broadcasted_iota(jnp.int32, (NB, side), 1) < start + NB
    kh, kl = halves(jnp.where(kept, fresh, 0.0))
    pair[0:NB, :] = kh
    pair[NB : 2 * NB, :] = kl


def kernel(
    lanes, rc_ref, cc_ref, g_in, l_in, r_in, out,
    gm, gbuf, pbuf, s_ref, w_ref, x_ref, a_ref, lcat, rcat, pair, m_ref, d_ref,
    ssem, gsem, psem, osem, xsend, xrecv, xown,
):
    me = lax.axis_index("tensor")
    block = lax.axis_index("fsdp")
    rows, side = g_in.shape
    steps = side // NB
    tile = min(256, side)
    left, right = workers(lanes)
    ring_barrier(lanes, me)

    def rows_of(lane):
        return pl.ds(pl.multiple_of(lane * rows, rows), rows)

    mine = rows_of(me)
    rid = me * rows + lax.broadcasted_iota(jnp.int32, (rows, side), 0)
    cid = lax.broadcasted_iota(jnp.int32, (rows, side), 1)
    keep = (rid < rc_ref[block]) & (cid < cc_ref[block])
    gm[...] = jnp.where(keep, g_in[...].astype(F32), 0.0).astype(BF16)

    def remote(src, dst, k, sem, to):
        return pltpu.make_async_remote_copy(
            src_ref=src, dst_ref=dst.at[mine], send_sem=ssem.at[k], recv_sem=sem.at[me],
            device_id={"tensor": to}, device_id_type=MESH,
        )

    jobs = (
        (left, gm, gbuf, 0, gsem), (right, gm, gbuf, 1, gsem), (left, l_in, pbuf, 2, psem), (right, r_in, pbuf, 3, psem)
    )
    for to, src, dst, k, sem in jobs:
        @pl.when(me != to)
        def _():
            remote(src, dst, k, sem, to).start()

        @pl.when(me == to)
        def _():
            pltpu.make_async_copy(src, dst.at[mine], osem.at[k]).start()

    def finish_jobs(chosen):
        for to, src, dst, k, sem in chosen:
            @pl.when(me != to)
            def _():
                remote(src, dst, k, sem, to).wait_send()

            @pl.when(me == to)
            def _():
                pltpu.make_async_copy(src, dst.at[mine], osem.at[k]).wait()

    def arrived(src, dst, sem):
        for step in range(1, lanes):
            other = lax.rem(me + step, lanes)
            pltpu.make_async_remote_copy(
                src_ref=src, dst_ref=dst.at[rows_of(other)], send_sem=ssem.at[0], recv_sem=sem.at[other],
                device_id={"tensor": other}, device_id_type=MESH,
            ).wait_recv()

    def columns(step):
        return pl.ds(pl.multiple_of(step * NB, NB), NB)

    def give(which, step, turn):
        other = lax.rem(me + turn, lanes)
        return pltpu.make_async_remote_copy(
            src_ref=x_ref.at[rows_of(other), columns(step)], dst_ref=out.at[which, :, columns(step)],
            send_sem=xsend.at[step, turn], recv_sem=xrecv.at[which, step],
            device_id={"tensor": other}, device_id_type=MESH,
        )

    def own(which, step):
        return pltpu.make_async_copy(x_ref.at[mine, columns(step)], out.at[which, :, columns(step)], xown.at[step])

    def result(step, which):
        both = nt(w_ref[...], pair[...])
        x_ref[:, columns(step)] = (both[:, :NB] + both[:, NB:]).astype(BF16)
        for turn in range(1, lanes):
            give(which, step, turn).start()
        own(which, step).start()

    def at(t):
        return pl.ds(pl.multiple_of(t * tile, tile), tile)

    def next_diag(step):
        later = columns(lax.rem(step + 1, steps))
        mh, ml = halves(m_ref[...])
        ch, cl = halves(a_ref[later, columns(step)])
        low = nt(jnp.concatenate([ch, cl, ch], axis=1), jnp.concatenate([mh, mh, ml], axis=1))
        lh, ll = halves(low)
        d_ref[...] = a_ref[later, later] - nt(
            jnp.concatenate([lh, ll, lh], axis=1), jnp.concatenate([lh, lh, ll], axis=1)
        )

    def begin(which):
        finish_jobs(jobs[which : which + 1])
        arrived(gm, gbuf, gsem)

        @pl.loop(0, side // tile)
        def _(t):
            if which == 0:
                stat = nt(gbuf[at(t), :], gbuf[...])
            else:
                stat = tn(gbuf[:, at(t)], gbuf[...])
            s_ref[at(t), :] = (stat * (1.0 / side)).astype(BF16)

        finish_jobs(jobs[2 + which : 3 + which])
        arrived(l_in, pbuf, psem)
        finish_jobs((jobs[1 - which], jobs[3 - which]))

    for which, worker in enumerate((left, right)):
        @pl.when(me == worker)
        def _():
            begin(which)

    working = (me == left) | (me == right)
    side_of = lax.div(lax.rem(me - left + lanes, lanes), lanes // 2)

    @pl.when(working)
    def _():
        @pl.loop(0, side // tile)
        def _(t):
            w_ref[at(t), :] = (nn(s_ref[at(t), :], pbuf[...]) + pbuf[at(t), :].astype(F32)).astype(BF16)

        @pl.loop(0, side // tile)
        def _(t):
            a_ref[at(t), :] = tn(w_ref[:, at(t)], w_ref[...])

        d_ref[...] = a_ref[0:NB, 0:NB]

        def invert():
            for i, part in enumerate(diag_inverse(lambda i: d_ref[8 * i : 8 * i + 8, :])):
                m_ref[8 * i : 8 * i + 8, :] = part

        invert()
        next_diag(0)

        @pl.loop(1, steps)
        def _(step):
            eliminate(step - 1, a_ref, m_ref, lcat, rcat, pair)
            result(step - 1, side_of)
            invert()
            next_diag(step)

        mh, ml = halves(m_ref[...])
        scale_row(steps - 1, a_ref, m_ref, mh, ml, rcat, pair)
        result(steps - 1, side_of)

        @pl.loop(0, steps)
        def _(step):
            for turn in range(1, lanes):
                give(side_of, step, turn).wait_send()
            own(side_of, step).wait()

    @pl.when(jnp.logical_not(working))
    def _():
        finish_jobs(jobs)

    for which, worker in enumerate((left, right)):
        @pl.when(me != worker)
        def _():
            @pl.loop(0, steps)
            def _(step):
                give(which, step, 1).wait_recv()


def hand_on(both, c, d, sem):
    first = pltpu.make_async_copy(both.at[0], c, sem.at[0])
    second = pltpu.make_async_copy(both.at[1], d, sem.at[1])
    first.start()
    second.start()
    first.wait()
    second.wait()


def body(grads, row_counts, col_counts, old_left, old_right):
    rows, side = grads.shape[1:]
    lanes = lax.axis_size("tensor")
    steps = side // NB
    vmem = pl.BlockSpec(memory_space=pltpu.VMEM)
    smem = pl.BlockSpec(memory_space=pltpu.SMEM)
    hbm = pl.BlockSpec(memory_space=pl.ANY)
    part = jax.ShapeDtypeStruct((rows, side), BF16)
    dma = pltpu.SemaphoreType.DMA
    whole = pltpu.VMEM((side, side), BF16)
    square = pltpu.VMEM((NB, NB), F32)
    both = pl.pallas_call(
        functools.partial(kernel, lanes),
        out_shape=jax.ShapeDtypeStruct((2, rows, side), BF16),
        in_specs=[smem, smem, vmem, vmem, vmem],
        out_specs=hbm,
        scratch_shapes=[
            pltpu.VMEM((rows, side), BF16),
            whole, whole, whole, whole, whole,
            pltpu.VMEM((side, side), F32),
            pltpu.VMEM((side, 3 * NB), BF16),
            pltpu.VMEM((3 * NB, side), BF16),
            pltpu.VMEM((2 * NB, side), BF16),
            square, square,
            dma((4,)), dma((lanes,)), dma((lanes,)), dma((4,)),
            dma((steps, lanes)), dma((2, steps)), dma((steps,)),
        ],
        compiler_params=pltpu.CompilerParams(
            collective_id=0, has_side_effects=True, vmem_limit_bytes=VMEM_LIMIT
        ),
        cost_estimate=pl.CostEstimate(flops=14 * side**3, bytes_accessed=6 * side * side, transcendentals=0),
        name="refresh",
    )(row_counts, col_counts, grads[0], old_left[0], old_right[0])
    new_left, new_right = pl.pallas_call(
        hand_on,
        out_shape=(part, part),
        in_specs=[hbm],
        out_specs=(hbm, hbm),
        scratch_shapes=[dma((2,))],
        name="hand_on",
    )(both)
    return (new_left[None], new_right[None])


def solution(mesh):
    split = P("fsdp", "tensor", None)
    return jax.shard_map(
        body, mesh=mesh, in_specs=(split, P(), P(), split, split), out_specs=(split, split), check_vma=False
    )
```

time: 141 us -> 136 us (0.965)
  local copies, waits for them, and re-layouts: 3.34 us -> 0 us
  Pallas kernels: 137 us -> 135 us
    unnamed x2 -> x0, local copies, waits for them, and re-layouts: 3.34 us -> none
    pallas_call x3 -> x2, Pallas kernels: 137 us -> 135 us  [the longest x1 118 us: body(): pl.pallas_call(functools.partial(kernel, lanes), out_shape=jax.ShapeDtype...]
where the time goes in v2:
time: 136 us
  Pallas kernels  135 us (99%)
    pallas_call x1, Pallas kernels, body(): pl.pallas_call(functools.partial(kernel, lanes), out_shape=jax.ShapeDtype...  118 us
    pallas_call x1, Pallas kernels, body(): pl.pallas_call(hand_on, out_shape=(part, part), in_specs=[hbm], out_specs...  17 us

profile of v2, /device:TPU:6, one launch (start us, length us, event | category | flops | bytes accessed | tf_op | source)
XLA Modules:
  0.0 135.8 jit_solution(8334433419409674941)
XLA Ops:
  0.6 118.2 %refresh.1.both = bf16[2,128,1024]{2,1,0:T(8,128)(2,1)} custom-call(s32[64]{0:T(128)} %rc_ref.1, s32[64]{0:T(128)} %cc_ref.1, bf16[128,1024]{1,0:T(8,128)(2,1)} %bitcast.5, bf16[128,1024]{1,0:T(8,128)(2,1)} %bitcast.6, bf16[128,1024]{1,0:T(8,128)(2,1)} %bitcast.7), custom_call_target="tpu_custom_call" | custom-call | flops 15032385536 | bytes 6291456 | tf_op jit(solution)/shard_map/refresh/pallas_call | solution.py:325
  118.8 17.0 %hand_on.1 = (bf16[128,1024]{1,0:T(8,128)(2,1)}, bf16[128,1024]{1,0:T(8,128)(2,1)}) custom-call(bf16[2,128,1024]{2,1,0:T(8,128)(2,1)} %refresh.1.both), custom_call_target="tpu_custom_call" | custom-call | tf_op jit(solution)/shard_map/hand_on/pallas_call | solution.py:347

commit v3 on v2

--- a/solution.py
+++ b/solution.py
@@ -37,46 +37,75 @@
     return r * (2.0 - x * r)
 
 
-def diag_inverse(load):
+def group_update(body, inside, k0, rcp, upper, flat):
+    cols = [across(body[:, k0 + q : k0 + q + 1]) for q in range(8)]
+    body = jnp.where(inside, 0.0, body)
+    for p in range(8):
+        w = cols[p] * rcp[p]
+        for q in range(p + 1, 8):
+            cols[q] = cols[q] - w * upper[p][q]
+        body = body - w * flat[p]
+    return body
+
+
+def diag_rounds(load, store):
     count = NB // 8
     sub = lax.broadcasted_iota(jnp.int32, (8, NB), 0)
     lane = lax.broadcasted_iota(jnp.int32, (8, NB), 1)
     rows = [load(i) for i in range(count)]
-    done = []
     for r in range(count):
         k0 = 8 * r
         inside = (lane >= k0) & (lane < k0 + 8)
         top = rows[r]
         cols = [across(top[:, k0 + q : k0 + q + 1]) for q in range(8)]
+        u = [{q: across(cols[q][p : p + 1, :]) for q in range(p, 8)} for p in range(8)]
         top = jnp.where(lane - k0 == sub, 1.0, jnp.where(inside, 0.0, top))
-        rcp, upper, flat = [], [], []
-        scale = jnp.zeros((8, NB), F32)
+        flat = [across(top[p : p + 1, :]) for p in range(8)]
+        rcp = [None] * 8
+        root = [None] * 8
+        for p in range(0, 8, 2):
+            n = p + 1
+            det = u[p][p] * u[n][n] - u[p][n] * u[p][n]
+            rcp[p] = inverse_rcp(u[p][p])
+            rcp[n] = u[p][p] * inverse_rcp(det)
+            root[p] = lax.rsqrt(u[p][p])
+            root[n] = lax.rsqrt(det * rcp[p])
+            low = {s: u[p][s] * rcp[p] for s in range(n, 8)}
+            for t in range(n + 1, 8):
+                u[n][t] = u[n][t] - low[n] * u[p][t]
+            high = {s: u[n][s] * rcp[n] for s in range(n + 1, 8)}
+            for s in range(n + 1, 8):
+                for t in range(s, 8):
+                    u[s][t] = u[s][t] - low[s] * u[p][t] - high[s] * u[n][t]
+            flat[n] = flat[n] - low[n] * flat[p]
+            for s in range(n + 1, 8):
+                flat[s] = flat[s] - low[s] * flat[p] - high[s] * flat[n]
+        for i in range(r + 1, min(r + 3, count)):
+            rows[i] = group_update(rows[i], inside, k0, rcp, u, flat)
+        scaled = jnp.zeros((8, NB), F32)
         for p in range(8):
-            pivot = across(cols[p][p : p + 1, :])
-            inv = inverse_rcp(pivot)
-            scale = jnp.where(sub == p, lax.rsqrt(pivot), scale)
-            mult = jnp.where(sub > p, cols[p] * inv, 0.0)
-            line = {}
-            for q in range(p + 1, 8):
-                line[q] = across(cols[q][p : p + 1, :])
-                cols[q] = cols[q] - mult * line[q]
-            row = across(top[p : p + 1, :])
-            top = top - mult * row
-            rcp.append(inv)
-            upper.append(line)
-            flat.append(row)
-        done.append(jnp.where(lane <= sub + k0, top * scale, 0.0))
-        for i in range(r + 1, count):
-            body = rows[i]
-            cols = [across(body[:, k0 + q : k0 + q + 1]) for q in range(8)]
-            body = jnp.where(inside, 0.0, body)
-            for p in range(8):
-                w = cols[p] * rcp[p]
-                for q in range(p + 1, 8):
-                    cols[q] = cols[q] - w * upper[p][q]
-                body = body - w * flat[p]
-            rows[i] = body
-    return done
+            scaled = jnp.where(sub == p, flat[p] * root[p], scaled)
+        store(r, jnp.where(lane <= sub + k0, scaled, 0.0))
+        if r + 3 < count:
+            high = scaled.astype(BF16).astype(F32)
+            low = scaled - high
+            zero = jnp.zeros((8, NB), F32)
+            left = jnp.concatenate([high, low, high, zero], axis=0).astype(BF16)
+            right = jnp.concatenate([high, high, low, zero], axis=0).astype(BF16)
+            off = tn(left, right)
+            for i in range(r + 3, count):
+                rows[i] = jnp.where(inside, 0.0, rows[i]) - off[8 * i : 8 * i + 8, :]
+        yield
+
+
+def weave(rounds, chunks):
+    chunks = list(chunks)
+    total, rounds_total, given = len(chunks), NB // 8, 0
+    for done, _ in enumerate(rounds, 1):
+        upto = total * done // rounds_total
+        for chunk in chunks[given:upto]:
+            chunk()
+        given = upto
 
 
 def halves(x):
@@ -100,21 +129,30 @@
     side = a_ref.shape[0]
     start = pl.multiple_of(step * NB, NB)
     here = pl.ds(start, NB)
-    mh, ml = halves(m_ref[...])
-    scale_row(step, a_ref, m_ref, mh, ml, rcat, pair)
-    below = lax.broadcasted_iota(jnp.int32, (side, NB), 0) >= start + NB
-    column = a_ref[:, here]
-    ch, cl = halves(jnp.where(below, column, 0.0))
-    low = nt(jnp.concatenate([ch, cl, ch], axis=1), jnp.concatenate([mh, mh, ml], axis=1))
-    lh, ll = halves(low)
-    lcat[:, 0:NB] = lh
-    lcat[:, NB : 2 * NB] = ll
-    lcat[:, 2 * NB : 3 * NB] = lh
-    a_ref[:, here] = jnp.where(below, 0.0, column)
     tile = min(256, side)
-    for t in range(side // tile):
-        cols = slice(t * tile, (t + 1) * tile)
-        a_ref[:, cols] = a_ref[:, cols] - nn(lcat[...], rcat[:, cols])
+    spans = [slice(t * tile, (t + 1) * tile) for t in range(side // tile)]
+
+    def scale():
+        mh, ml = halves(m_ref[...])
+        scale_row(step, a_ref, m_ref, mh, ml, rcat, pair)
+
+    def multiples(span):
+        mh, ml = halves(m_ref[...])
+        below = span.start + lax.broadcasted_iota(jnp.int32, (tile, NB), 0) >= start + NB
+        column = a_ref[span, here]
+        ch, cl = halves(jnp.where(below, column, 0.0))
+        low = nt(jnp.concatenate([ch, cl, ch], axis=1), jnp.concatenate([mh, mh, ml], axis=1))
+        lh, ll = halves(low)
+        lcat[span, 0:NB] = lh
+        lcat[span, NB : 2 * NB] = ll
+        lcat[span, 2 * NB : 3 * NB] = lh
+        a_ref[span, here] = jnp.where(below, 0.0, column)
+
+    def trail(rows, cols):
+        a_ref[rows, cols] = a_ref[rows, cols] - nn(lcat[rows, :], rcat[:, cols])
+
+    pieces = [scale] + [functools.partial(multiples, span) for span in spans]
+    return pieces + [functools.partial(trail, rows, cols) for cols in spans for rows in spans]
 
 
 def scale_row(step, a_ref, m_ref, mh, ml, rcat, pair):
@@ -210,12 +248,18 @@
     def own(which, step):
         return pltpu.make_async_copy(x_ref.at[mine, columns(step)], out.at[which, :, columns(step)], xown.at[step])
 
-    def result(step, which):
-        both = nt(w_ref[...], pair[...])
-        x_ref[:, columns(step)] = (both[:, :NB] + both[:, NB:]).astype(BF16)
+    def product(step):
+        def piece(t):
+            span = slice(t * tile, (t + 1) * tile)
+            both = nt(w_ref[span, :], pair[...])
+            x_ref[span, columns(step)] = (both[:, :NB] + both[:, NB:]).astype(BF16)
+
+        return [functools.partial(piece, t) for t in range(side // tile)]
+
+    def send(step):
         for turn in range(1, lanes):
-            give(which, step, turn).start()
-        own(which, step).start()
+            give(side_of, step, turn).start()
+        own(side_of, step).start()
 
     def at(t):
         return pl.ds(pl.multiple_of(t * tile, tile), tile)
@@ -260,29 +304,33 @@
         def _(t):
             w_ref[at(t), :] = (nn(s_ref[at(t), :], pbuf[...]) + pbuf[at(t), :].astype(F32)).astype(BF16)
 
-        @pl.loop(0, side // tile)
-        def _(t):
-            a_ref[at(t), :] = tn(w_ref[:, at(t)], w_ref[...])
-
-        d_ref[...] = a_ref[0:NB, 0:NB]
-
-        def invert():
-            for i, part in enumerate(diag_inverse(lambda i: d_ref[8 * i : 8 * i + 8, :])):
+        d_ref[...] = tn(w_ref[:, 0:NB], w_ref[:, 0:NB])
+
+        def invert(chunks):
+            parts = []
+            rounds = diag_rounds(lambda i: d_ref[8 * i : 8 * i + 8, :], lambda i, part: parts.append(part))
+            weave(rounds, chunks)
+            for i, part in enumerate(parts):
                 m_ref[8 * i : 8 * i + 8, :] = part
 
-        invert()
+        def gram(t):
+            span = slice(t * tile, (t + 1) * tile)
+            a_ref[span, :] = tn(w_ref[:, span], w_ref[...])
+
+        invert([functools.partial(gram, t) for t in range(side // tile)])
         next_diag(0)
 
         @pl.loop(1, steps)
         def _(step):
-            eliminate(step - 1, a_ref, m_ref, lcat, rcat, pair)
-            result(step - 1, side_of)
-            invert()
+            invert(eliminate(step - 1, a_ref, m_ref, lcat, rcat, pair) + product(step - 1))
             next_diag(step)
+            send(step - 1)
 
         mh, ml = halves(m_ref[...])
         scale_row(steps - 1, a_ref, m_ref, mh, ml, rcat, pair)
-        result(steps - 1, side_of)
+        for piece in product(steps - 1):
+            piece()
+        send(steps - 1)
 
         @pl.loop(0, steps)
         def _(step):
@@ -302,13 +350,9 @@
                 give(which, step, 1).wait_recv()
 
 
-def hand_on(both, c, d, sem):
-    first = pltpu.make_async_copy(both.at[0], c, sem.at[0])
-    second = pltpu.make_async_copy(both.at[1], d, sem.at[1])
-    first.start()
-    second.start()
-    first.wait()
-    second.wait()
+def hand_on(both, first, second):
+    first[...] = both[0]
+    second[...] = both[1]
 
 
 def body(grads, row_counts, col_counts, old_left, old_right):
@@ -347,9 +391,8 @@
     new_left, new_right = pl.pallas_call(
         hand_on,
         out_shape=(part, part),
-        in_specs=[hbm],
-        out_specs=(hbm, hbm),
-        scratch_shapes=[dma((2,))],
+        in_specs=[vmem],
+        out_specs=(vmem, vmem),
         name="hand_on",
     )(both)
     return (new_left[None], new_right[None])

time: 136 us -> 98.7 us (0.73)
  Pallas kernels: 135 us -> 97.8 us
    pallas_call x1, Pallas kernels: 118 us -> 96 us  [body(): pl.pallas_call(functools.partial(kernel, lanes), out_shape=jax.ShapeDtype...]
    pallas_call x1, Pallas kernels: 17 us -> 1.85 us  [body(): pl.pallas_call(hand_on, out_shape=(part, part), in_specs=[vmem], out_spec...]
where the time goes in v3:
time: 98.7 us; the launch traced here: 98.5 us
  Pallas kernels  97.8 us (99%)
    pallas_call x1, Pallas kernels, body(): pl.pallas_call(functools.partial(kernel, lanes), out_shape=jax.ShapeDtype...  96 us

profile of v3, /device:TPU:6, one launch (start us, length us, event | category | flops | bytes accessed | tf_op | source)
XLA Modules:
  0.0 98.5 jit_solution(1887886397800564161)
XLA Ops:
  0.6 96.0 %refresh.1.both = bf16[2,128,1024]{2,1,0:T(8,128)(2,1)} custom-call(s32[64]{0:T(128)} %rc_ref.1, s32[64]{0:T(128)} %cc_ref.1, bf16[128,1024]{1,0:T(8,128)(2,1)} %bitcast.5, bf16[128,1024]{1,0:T(8,128)(2,1)} %bitcast.6, bf16[128,1024]{1,0:T(8,128)(2,1)} %bitcast.7), custom_call_target="tpu_custom_call" | custom-call | flops 15032385536 | bytes 6291456 | tf_op jit(solution)/shard_map/refresh/pallas_call | solution.py:369
  96.6 1.8 %hand_on.1 = (bf16[128,1024]{1,0:T(8,128)(2,1)}, bf16[128,1024]{1,0:T(8,128)(2,1)}) custom-call(bf16[2,128,1024]{2,1,0:T(8,128)(2,1)} %refresh.1.both), custom_call_target="tpu_custom_call" | custom-call | tf_op jit(solution)/shard_map/hand_on/pallas_call | solution.py:391

commit v4 on v3

--- a/solution.py
+++ b/solution.py
@@ -20,11 +20,12 @@
     return left, left + lanes // 2
 
 
-def ring_barrier(lanes, me):
+def ring_barrier(lanes, me, meanwhile):
     barrier = pltpu.get_barrier_semaphore()
     for step in range(1, lanes):
         other = lax.rem(me + step, lanes)
         pl.semaphore_signal(barrier, inc=1, device_id={"tensor": other}, device_id_type=MESH)
+    meanwhile()
     pl.semaphore_wait(barrier, lanes - 1)
 
 
@@ -125,7 +126,7 @@
     return lax.dot_general(a, b, (((0,), (0,)), ((), ())), preferred_element_type=F32)
 
 
-def eliminate(step, a_ref, m_ref, lcat, rcat, pair):
+def eliminate(step, phase, a_ref, m_ref, lcat, rcat, pair):
     side = a_ref.shape[0]
     start = pl.multiple_of(step * NB, NB)
     here = pl.ds(start, NB)
@@ -151,8 +152,8 @@
     def trail(rows, cols):
         a_ref[rows, cols] = a_ref[rows, cols] - nn(lcat[rows, :], rcat[:, cols])
 
-    pieces = [scale] + [functools.partial(multiples, span) for span in spans]
-    return pieces + [functools.partial(trail, rows, cols) for cols in spans for rows in spans]
+    pieces = [scale] + [functools.partial(multiples, span) for span in spans[phase:]]
+    return pieces + [functools.partial(trail, rows, cols) for cols in spans for rows in spans[phase:]]
 
 
 def scale_row(step, a_ref, m_ref, mh, ml, rcat, pair):
@@ -187,16 +188,18 @@
     steps = side // NB
     tile = min(256, side)
     left, right = workers(lanes)
-    ring_barrier(lanes, me)
-
     def rows_of(lane):
         return pl.ds(pl.multiple_of(lane * rows, rows), rows)
 
     mine = rows_of(me)
-    rid = me * rows + lax.broadcasted_iota(jnp.int32, (rows, side), 0)
-    cid = lax.broadcasted_iota(jnp.int32, (rows, side), 1)
-    keep = (rid < rc_ref[block]) & (cid < cc_ref[block])
-    gm[...] = jnp.where(keep, g_in[...].astype(F32), 0.0).astype(BF16)
+
+    def mask():
+        rid = me * rows + lax.broadcasted_iota(jnp.int32, (rows, side), 0)
+        cid = lax.broadcasted_iota(jnp.int32, (rows, side), 1)
+        keep = (rid < rc_ref[block]) & (cid < cc_ref[block])
+        gm[...] = jnp.where(keep, g_in[...].astype(F32), 0.0).astype(BF16)
+
+    ring_barrier(lanes, me, mask)
 
     def remote(src, dst, k, sem, to):
         return pltpu.make_async_remote_copy(
@@ -248,13 +251,36 @@
     def own(which, step):
         return pltpu.make_async_copy(x_ref.at[mine, columns(step)], out.at[which, :, columns(step)], xown.at[step])
 
-    def product(step):
+    def pair_product(t, depth):
+        both = nt(w_ref[t * tile : (t + 1) * tile, :depth], pair[:, :depth])
+        return both[:, :NB] + both[:, NB:]
+
+    def product(step, phase):
+        def piece(t):
+            x_ref[t * tile : (t + 1) * tile, columns(step)] = pair_product(t, tile * (phase + 1)).astype(BF16)
+
+        return [functools.partial(piece, t) for t in range(side // tile)]
+
+    def unscaled_last():
+        last = slice(side - NB, side)
+
+        def rows():
+            eye = lax.broadcasted_iota(jnp.int32, (NB, NB), 0) == lax.broadcasted_iota(jnp.int32, (NB, NB), 1)
+            pair[0:NB, last] = jnp.where(eye, 1.0, 0.0).astype(BF16)
+            pair[NB:, last] = jnp.zeros((NB, NB), BF16)
+            if side > NB:
+                high, low = halves(a_ref[last, : side - NB])
+                pair[0:NB, : side - NB] = high
+                pair[NB:, : side - NB] = low
+
         def piece(t):
             span = slice(t * tile, (t + 1) * tile)
-            both = nt(w_ref[span, :], pair[...])
-            x_ref[span, columns(step)] = (both[:, :NB] + both[:, NB:]).astype(BF16)
-
-        return [functools.partial(piece, t) for t in range(side // tile)]
+            high, low = halves(pair_product(t, side))
+            lcat[span, 0:NB] = high
+            lcat[span, NB : 2 * NB] = low
+            lcat[span, 2 * NB :] = high
+
+        return [rows] + [functools.partial(piece, t) for t in range(side // tile)]
 
     def send(step):
         for turn in range(1, lanes):
@@ -320,17 +346,25 @@
         invert([functools.partial(gram, t) for t in range(side // tile)])
         next_diag(0)
 
-        @pl.loop(1, steps)
-        def _(step):
-            invert(eliminate(step - 1, a_ref, m_ref, lcat, rcat, pair) + product(step - 1))
-            next_diag(step)
-            send(step - 1)
-
+        each = tile // NB
+        for phase in range(side // tile - 1 if side > tile else 0):
+            @pl.loop(each * phase + 1, min(each * (phase + 1) + 1, steps - 1))
+            def _(step):
+                invert(eliminate(step - 1, phase, a_ref, m_ref, lcat, rcat, pair) + product(step - 1, phase))
+                next_diag(step)
+                send(step - 1)
+
+        phase = side // tile - 1
+        last = steps - 1
+        invert(
+            eliminate(last - 1, phase, a_ref, m_ref, lcat, rcat, pair) + product(last - 1, phase) + unscaled_last()
+        )
+        send(last - 1)
         mh, ml = halves(m_ref[...])
-        scale_row(steps - 1, a_ref, m_ref, mh, ml, rcat, pair)
-        for piece in product(steps - 1):
-            piece()
-        send(steps - 1)
+        for t in range(side // tile):
+            span = slice(t * tile, (t + 1) * tile)
+            x_ref[span, columns(last)] = nt(lcat[span, :], jnp.concatenate([mh, mh, ml], axis=1)).astype(BF16)
+        send(last)
 
         @pl.loop(0, steps)
         def _(step):

time: 98.7 us -> 97 us (0.983)
  Pallas kernels: 97.8 us -> 96.1 us
    pallas_call x1, Pallas kernels: 96 us -> 94.3 us  [body(): pl.pallas_call(functools.partial(kernel, lanes), out_shape=jax.ShapeDtype...]
where the time goes in v4:
time: 97 us; the launch traced here: 96.8 us
  Pallas kernels  96.1 us (99%)
    pallas_call x1, Pallas kernels, body(): pl.pallas_call(functools.partial(kernel, lanes), out_shape=jax.ShapeDtype...  94.3 us

profile of v4, /device:TPU:6, one launch (start us, length us, event | category | flops | bytes accessed | tf_op | source)
XLA Modules:
  0.0 96.8 jit_solution(7810190733540466707)
XLA Ops:
  0.6 94.3 %refresh.1.both = bf16[2,128,1024]{2,1,0:T(8,128)(2,1)} custom-call(s32[64]{0:T(128)} %rc_ref.1, s32[64]{0:T(128)} %cc_ref.1, bf16[128,1024]{1,0:T(8,128)(2,1)} %bitcast.5, bf16[128,1024]{1,0:T(8,128)(2,1)} %bitcast.6, bf16[128,1024]{1,0:T(8,128)(2,1)} %bitcast.7), custom_call_target="tpu_custom_call" | custom-call | flops 15032385536 | bytes 6291456 | tf_op jit(solution)/shard_map/refresh/pallas_call | solution.py:403
  94.9 1.8 %hand_on.1 = (bf16[128,1024]{1,0:T(8,128)(2,1)}, bf16[128,1024]{1,0:T(8,128)(2,1)}) custom-call(bf16[2,128,1024]{2,1,0:T(8,128)(2,1)} %refresh.1.both), custom_call_target="tpu_custom_call" | custom-call | tf_op jit(solution)/shard_map/hand_on/pallas_call | solution.py:425

commit v5 on v4

--- a/solution.py
+++ b/solution.py
@@ -11,6 +11,7 @@
 BF16 = jnp.bfloat16
 F32 = jnp.float32
 NB = 128
+NEAR = 3
 VMEM_LIMIT = 56 * 1024 * 1024
 
 
@@ -49,7 +50,7 @@
     return body
 
 
-def diag_rounds(load, store):
+def diag_rounds(load, store, lines):
     count = NB // 8
     sub = lax.broadcasted_iota(jnp.int32, (8, NB), 0)
     lane = lax.broadcasted_iota(jnp.int32, (8, NB), 1)
@@ -57,44 +58,47 @@
     for r in range(count):
         k0 = 8 * r
         inside = (lane >= k0) & (lane < k0 + 8)
-        top = rows[r]
-        cols = [across(top[:, k0 + q : k0 + q + 1]) for q in range(8)]
-        u = [{q: across(cols[q][p : p + 1, :]) for q in range(p, 8)} for p in range(8)]
-        top = jnp.where(lane - k0 == sub, 1.0, jnp.where(inside, 0.0, top))
-        flat = [across(top[p : p + 1, :]) for p in range(8)]
+        lines[8 * r : 8 * r + 8, :] = rows[r]
+        flat = [across(lines[k0 + p : k0 + p + 1, :]) for p in range(8)]
+        u = [{q: across(flat[p][:, k0 + q : k0 + q + 1]) for q in range(p, 8)} for p in range(8)]
+        flat = [jnp.where(lane == k0 + p, 1.0, jnp.where(inside, 0.0, flat[p])) for p in range(8)]
         rcp = [None] * 8
         root = [None] * 8
         for p in range(0, 8, 2):
             n = p + 1
-            det = u[p][p] * u[n][n] - u[p][n] * u[p][n]
-            rcp[p] = inverse_rcp(u[p][p])
-            rcp[n] = u[p][p] * inverse_rcp(det)
-            root[p] = lax.rsqrt(u[p][p])
+            a, b, c = u[p][p], u[p][n], u[n][n]
+            det = a * c - b * b
+            guess = pl.reciprocal(det, approx=True)
+            fix = 2.0 - det * guess
+            for s in range(n + 1, 8):
+                g = c * u[p][s] - b * u[n][s]
+                h = a * u[n][s] - b * u[p][s]
+                for t in range(s, 8):
+                    u[s][t] = u[s][t] - ((g * u[p][t] + h * u[n][t]) * guess) * fix
+            rcp[p] = inverse_rcp(a)
+            rcp[n] = a * (guess * fix)
+            root[p] = lax.rsqrt(a)
             root[n] = lax.rsqrt(det * rcp[p])
             low = {s: u[p][s] * rcp[p] for s in range(n, 8)}
             for t in range(n + 1, 8):
                 u[n][t] = u[n][t] - low[n] * u[p][t]
-            high = {s: u[n][s] * rcp[n] for s in range(n + 1, 8)}
-            for s in range(n + 1, 8):
-                for t in range(s, 8):
-                    u[s][t] = u[s][t] - low[s] * u[p][t] - high[s] * u[n][t]
             flat[n] = flat[n] - low[n] * flat[p]
             for s in range(n + 1, 8):
-                flat[s] = flat[s] - low[s] * flat[p] - high[s] * flat[n]
-        for i in range(r + 1, min(r + 3, count)):
+                flat[s] = flat[s] - low[s] * flat[p] - (u[n][s] * rcp[n]) * flat[n]
+        for i in range(r + 1, min(r + 1 + NEAR, count)):
             rows[i] = group_update(rows[i], inside, k0, rcp, u, flat)
         scaled = jnp.zeros((8, NB), F32)
         for p in range(8):
             scaled = jnp.where(sub == p, flat[p] * root[p], scaled)
         store(r, jnp.where(lane <= sub + k0, scaled, 0.0))
-        if r + 3 < count:
+        if r + 1 + NEAR < count:
             high = scaled.astype(BF16).astype(F32)
             low = scaled - high
             zero = jnp.zeros((8, NB), F32)
             left = jnp.concatenate([high, low, high, zero], axis=0).astype(BF16)
             right = jnp.concatenate([high, high, low, zero], axis=0).astype(BF16)
             off = tn(left, right)
-            for i in range(r + 3, count):
+            for i in range(r + 1 + NEAR, count):
                 rows[i] = jnp.where(inside, 0.0, rows[i]) - off[8 * i : 8 * i + 8, :]
         yield
 
@@ -179,7 +183,7 @@
 
 def kernel(
     lanes, rc_ref, cc_ref, g_in, l_in, r_in, out,
-    gm, gbuf, pbuf, s_ref, w_ref, x_ref, a_ref, lcat, rcat, pair, m_ref, d_ref,
+    gm, gbuf, pbuf, s_ref, w_ref, x_ref, a_ref, lcat, rcat, pair, m_ref, d_ref, lines,
     ssem, gsem, psem, osem, xsend, xrecv, xown,
 ):
     me = lax.axis_index("tensor")
@@ -334,7 +338,7 @@
 
         def invert(chunks):
             parts = []
-            rounds = diag_rounds(lambda i: d_ref[8 * i : 8 * i + 8, :], lambda i, part: parts.append(part))
+            rounds = diag_rounds(lambda i: d_ref[8 * i : 8 * i + 8, :], lambda i, part: parts.append(part), lines)
             weave(rounds, chunks)
             for i, part in enumerate(parts):
                 m_ref[8 * i : 8 * i + 8, :] = part
@@ -412,7 +416,7 @@
             pltpu.VMEM((side, 3 * NB), BF16),
             pltpu.VMEM((3 * NB, side), BF16),
             pltpu.VMEM((2 * NB, side), BF16),
-            square, square,
+            square, square, square,
             dma((4,)), dma((lanes,)), dma((lanes,)), dma((4,)),
             dma((steps, lanes)), dma((2, steps)), dma((steps,)),
         ],

time: 97 us -> 97 us (level)
  no operation moved by 1% of the time
where the time goes in v5:
time: 97 us; the launch traced here: 96.8 us
  Pallas kernels  96.2 us (99%)
    pallas_call x1, Pallas kernels, body(): pl.pallas_call(functools.partial(kernel, lanes), out_shape=jax.ShapeDtype...  94.3 us

profile of v5, /device:TPU:6, one launch (start us, length us, event | category | flops | bytes accessed | tf_op | source)
XLA Modules:
  0.0 96.8 jit_solution(360998380875922176)
XLA Ops:
  0.6 94.3 %refresh.1.both = bf16[2,128,1024]{2,1,0:T(8,128)(2,1)} custom-call(s32[64]{0:T(128)} %rc_ref.1, s32[64]{0:T(128)} %cc_ref.1, bf16[128,1024]{1,0:T(8,128)(2,1)} %bitcast.5, bf16[128,1024]{1,0:T(8,128)(2,1)} %bitcast.6, bf16[128,1024]{1,0:T(8,128)(2,1)} %bitcast.7), custom_call_target="tpu_custom_call" | custom-call | flops 15032385536 | bytes 6291456 | tf_op jit(solution)/shard_map/refresh/pallas_call | solution.py:407
  95.0 1.8 %hand_on.1 = (bf16[128,1024]{1,0:T(8,128)(2,1)}, bf16[128,1024]{1,0:T(8,128)(2,1)}) custom-call(bf16[2,128,1024]{2,1,0:T(8,128)(2,1)} %refresh.1.both), custom_call_target="tpu_custom_call" | custom-call | tf_op jit(solution)/shard_map/hand_on/pallas_call | solution.py:429

commit v6 on v5

--- a/solution.py
+++ b/solution.py
@@ -11,7 +11,7 @@
 BF16 = jnp.bfloat16
 F32 = jnp.float32
 NB = 128
-NEAR = 3
+PANEL = 32
 VMEM_LIMIT = 56 * 1024 * 1024
 
 
@@ -50,17 +50,18 @@
     return body
 
 
-def diag_rounds(load, store, lines):
-    count = NB // 8
+def panel_rounds(turn, q_ref):
+    groups, panel = NB // 8, PANEL // 8
     sub = lax.broadcasted_iota(jnp.int32, (8, NB), 0)
     lane = lax.broadcasted_iota(jnp.int32, (8, NB), 1)
-    rows = [load(i) for i in range(count)]
-    for r in range(count):
+    rows = [q_ref[8 * i : 8 * i + 8, :] for i in range(panel)]
+    done = []
+    for r in range(panel):
         k0 = 8 * r
         inside = (lane >= k0) & (lane < k0 + 8)
-        lines[8 * r : 8 * r + 8, :] = rows[r]
-        flat = [across(lines[k0 + p : k0 + p + 1, :]) for p in range(8)]
-        u = [{q: across(flat[p][:, k0 + q : k0 + q + 1]) for q in range(p, 8)} for p in range(8)]
+        flat = [across(rows[r][p : p + 1, :]) for p in range(8)]
+        cols = [across(rows[r][:, k0 + q : k0 + q + 1]) for q in range(8)]
+        u = [{q: across(cols[q][p : p + 1, :]) for q in range(p, 8)} for p in range(8)]
         flat = [jnp.where(lane == k0 + p, 1.0, jnp.where(inside, 0.0, flat[p])) for p in range(8)]
         rcp = [None] * 8
         root = [None] * 8
@@ -85,27 +86,33 @@
             flat[n] = flat[n] - low[n] * flat[p]
             for s in range(n + 1, 8):
                 flat[s] = flat[s] - low[s] * flat[p] - (u[n][s] * rcp[n]) * flat[n]
-        for i in range(r + 1, min(r + 1 + NEAR, count)):
+        for i in range(r + 1, panel):
             rows[i] = group_update(rows[i], inside, k0, rcp, u, flat)
         scaled = jnp.zeros((8, NB), F32)
         for p in range(8):
             scaled = jnp.where(sub == p, flat[p] * root[p], scaled)
-        store(r, jnp.where(lane <= sub + k0, scaled, 0.0))
-        if r + 1 + NEAR < count:
-            high = scaled.astype(BF16).astype(F32)
-            low = scaled - high
-            zero = jnp.zeros((8, NB), F32)
-            left = jnp.concatenate([high, low, high, zero], axis=0).astype(BF16)
-            right = jnp.concatenate([high, high, low, zero], axis=0).astype(BF16)
-            off = tn(left, right)
-            for i in range(r + 1 + NEAR, count):
-                rows[i] = jnp.where(inside, 0.0, rows[i]) - off[8 * i : 8 * i + 8, :]
+        done.append(jnp.where((lane < PANEL) & (lane > sub + k0), 0.0, scaled))
         yield
+    whole = jnp.concatenate(done, axis=0)
+    high = whole.astype(BF16).astype(F32)
+    low = whole - high
+    ahead = lax.broadcasted_iota(jnp.int32, (PANEL, NB), 1)
+    ahead = (ahead >= PANEL) & (ahead < NB - PANEL * turn)
+    left = jnp.concatenate([high, low, high], axis=0)
+    ahead = jnp.concatenate([ahead.astype(F32)] * 3, axis=0)
+    left = (left * ahead).astype(BF16)
+    right = jnp.concatenate([high, high, low], axis=0).astype(BF16)
+    off = tn(left, right)
+    for i in range(panel, groups):
+        rest = jnp.where(lane < PANEL, 0.0, q_ref[8 * i : 8 * i + 8, :]) - off[8 * i : 8 * i + 8, :]
+        q_ref[8 * (i - panel) : 8 * (i - panel) + 8, :] = pltpu.roll(rest, NB - PANEL, 1)
+    for r in range(panel):
+        place = groups - panel + r
+        q_ref[8 * place : 8 * place + 8, :] = pltpu.roll(done[r], NB - PANEL, 1)
 
 
 def weave(rounds, chunks):
-    chunks = list(chunks)
-    total, rounds_total, given = len(chunks), NB // 8, 0
+    total, rounds_total, given = len(chunks), PANEL // 8, 0
     for done, _ in enumerate(rounds, 1):
         upto = total * done // rounds_total
         for chunk in chunks[given:upto]:
@@ -130,34 +137,23 @@
     return lax.dot_general(a, b, (((0,), (0,)), ((), ())), preferred_element_type=F32)
 
 
-def eliminate(step, phase, a_ref, m_ref, lcat, rcat, pair):
+def scale_step(step, phase, a_ref, m_ref, lcat, rcat, pair):
     side = a_ref.shape[0]
     start = pl.multiple_of(step * NB, NB)
     here = pl.ds(start, NB)
     tile = min(256, side)
-    spans = [slice(t * tile, (t + 1) * tile) for t in range(side // tile)]
-
-    def scale():
-        mh, ml = halves(m_ref[...])
-        scale_row(step, a_ref, m_ref, mh, ml, rcat, pair)
-
-    def multiples(span):
-        mh, ml = halves(m_ref[...])
-        below = span.start + lax.broadcasted_iota(jnp.int32, (tile, NB), 0) >= start + NB
-        column = a_ref[span, here]
-        ch, cl = halves(jnp.where(below, column, 0.0))
-        low = nt(jnp.concatenate([ch, cl, ch], axis=1), jnp.concatenate([mh, mh, ml], axis=1))
-        lh, ll = halves(low)
-        lcat[span, 0:NB] = lh
-        lcat[span, NB : 2 * NB] = ll
-        lcat[span, 2 * NB : 3 * NB] = lh
-        a_ref[span, here] = jnp.where(below, 0.0, column)
-
-    def trail(rows, cols):
-        a_ref[rows, cols] = a_ref[rows, cols] - nn(lcat[rows, :], rcat[:, cols])
-
-    pieces = [scale] + [functools.partial(multiples, span) for span in spans[phase:]]
-    return pieces + [functools.partial(trail, rows, cols) for cols in spans for rows in spans[phase:]]
+    span = slice(phase * tile, side)
+    mh, ml = halves(m_ref[...])
+    scale_row(step, a_ref, m_ref, mh, ml, rcat, pair)
+    below = phase * tile + lax.broadcasted_iota(jnp.int32, (side - phase * tile, NB), 0) >= start + NB
+    column = a_ref[span, here]
+    ch, cl = halves(jnp.where(below, column, 0.0))
+    low = nt(jnp.concatenate([ch, cl, ch], axis=1), jnp.concatenate([mh, mh, ml], axis=1))
+    lh, ll = halves(low)
+    lcat[span, 0:NB] = lh
+    lcat[span, NB : 2 * NB] = ll
+    lcat[span, 2 * NB : 3 * NB] = lh
+    a_ref[span, here] = jnp.where(below, 0.0, column)
 
 
 def scale_row(step, a_ref, m_ref, mh, ml, rcat, pair):
@@ -183,7 +179,7 @@
 
 def kernel(
     lanes, rc_ref, cc_ref, g_in, l_in, r_in, out,
-    gm, gbuf, pbuf, s_ref, w_ref, x_ref, a_ref, lcat, rcat, pair, m_ref, d_ref, lines,
+    gm, gbuf, pbuf, s_ref, w_ref, x_ref, a_ref, lcat, rcat, pair, pair2, m_ref, d_ref,
     ssem, gsem, psem, osem, xsend, xrecv, xown,
 ):
     me = lax.axis_index("tensor")
@@ -255,44 +251,39 @@
     def own(which, step):
         return pltpu.make_async_copy(x_ref.at[mine, columns(step)], out.at[which, :, columns(step)], xown.at[step])
 
-    def pair_product(t, depth):
-        both = nt(w_ref[t * tile : (t + 1) * tile, :depth], pair[:, :depth])
+    def at(t):
+        return pl.ds(pl.multiple_of(t * tile, tile), tile)
+
+    def pair_product(t, depth, rows):
+        both = nt(w_ref[at(t), :depth], rows[:, :depth])
         return both[:, :NB] + both[:, NB:]
 
-    def product(step, phase):
-        def piece(t):
-            x_ref[t * tile : (t + 1) * tile, columns(step)] = pair_product(t, tile * (phase + 1)).astype(BF16)
-
-        return [functools.partial(piece, t) for t in range(side // tile)]
-
-    def unscaled_last():
+    def product(t, step, phase):
+        x_ref[at(t), columns(step)] = pair_product(t, tile * (phase + 1), pair).astype(BF16)
+
+    def trail(t, first):
+        rows = slice(first * tile, (first + 1) * tile)
+        a_ref[rows, at(t)] = a_ref[rows, at(t)] - nn(lcat[rows, :], rcat[:, at(t)])
+
+    def last_rows():
         last = slice(side - NB, side)
-
-        def rows():
-            eye = lax.broadcasted_iota(jnp.int32, (NB, NB), 0) == lax.broadcasted_iota(jnp.int32, (NB, NB), 1)
-            pair[0:NB, last] = jnp.where(eye, 1.0, 0.0).astype(BF16)
-            pair[NB:, last] = jnp.zeros((NB, NB), BF16)
-            if side > NB:
-                high, low = halves(a_ref[last, : side - NB])
-                pair[0:NB, : side - NB] = high
-                pair[NB:, : side - NB] = low
-
-        def piece(t):
-            span = slice(t * tile, (t + 1) * tile)
-            high, low = halves(pair_product(t, side))
-            lcat[span, 0:NB] = high
-            lcat[span, NB : 2 * NB] = low
-            lcat[span, 2 * NB :] = high
-
-        return [rows] + [functools.partial(piece, t) for t in range(side // tile)]
+        eye = lax.broadcasted_iota(jnp.int32, (NB, NB), 0) == lax.broadcasted_iota(jnp.int32, (NB, NB), 1)
+        pair2[0:NB, last] = jnp.where(eye, 1.0, 0.0).astype(BF16)
+        pair2[NB:, last] = jnp.zeros((NB, NB), BF16)
+        high, low = halves(a_ref[last, : side - NB])
+        pair2[0:NB, : side - NB] = high
+        pair2[NB:, : side - NB] = low
+
+    def unscaled(t):
+        high, low = halves(pair_product(t, side, pair2))
+        lcat[at(t), 0:NB] = high
+        lcat[at(t), NB : 2 * NB] = low
+        lcat[at(t), 2 * NB :] = high
 
     def send(step):
         for turn in range(1, lanes):
             give(side_of, step, turn).start()
         own(side_of, step).start()
-
-    def at(t):
-        return pl.ds(pl.multiple_of(t * tile, tile), tile)
 
     def next_diag(step):
         later = columns(lax.rem(step + 1, steps))
@@ -337,35 +328,65 @@
         d_ref[...] = tn(w_ref[:, 0:NB], w_ref[:, 0:NB])
 
         def invert(chunks):
-            parts = []
-            rounds = diag_rounds(lambda i: d_ref[8 * i : 8 * i + 8, :], lambda i, part: parts.append(part), lines)
-            weave(rounds, chunks)
-            for i, part in enumerate(parts):
-                m_ref[8 * i : 8 * i + 8, :] = part
+            @pl.loop(0, NB // PANEL)
+            def _(t):
+                weave(panel_rounds(t, d_ref), chunks(t))
+
+            lower = lax.broadcasted_iota(jnp.int32, (NB, NB), 1) <= lax.broadcasted_iota(jnp.int32, (NB, NB), 0)
+            m_ref[...] = jnp.where(lower, d_ref[...], 0.0)
+
+        def some(count, work):
+            if count == NB // PANEL:
+                return lambda t: [functools.partial(work, t)]
+
+            def only(t):
+                @pl.when(t == 0)
+                def _():
+                    for k in range(count):
+                        work(k)
+
+            return lambda t: [functools.partial(only, t)]
 
         def gram(t):
-            span = slice(t * tile, (t + 1) * tile)
-            a_ref[span, :] = tn(w_ref[:, span], w_ref[...])
-
-        invert([functools.partial(gram, t) for t in range(side // tile)])
+            a_ref[at(t), :] = tn(w_ref[:, at(t)], w_ref[...])
+
+        tiles = side // tile
+        each = tile // NB
+        invert(some(tiles, gram))
         next_diag(0)
-
-        each = tile // NB
-        for phase in range(side // tile - 1 if side > tile else 0):
-            @pl.loop(each * phase + 1, min(each * (phase + 1) + 1, steps - 1))
-            def _(step):
-                invert(eliminate(step - 1, phase, a_ref, m_ref, lcat, rcat, pair) + product(step - 1, phase))
-                next_diag(step)
-                send(step - 1)
-
-        phase = side // tile - 1
+        scale_step(0, 0, a_ref, m_ref, lcat, rcat, pair)
+
+        def update(t, step, phase):
+            for first in range(phase, tiles):
+                trail(t, first)
+            product(t, step, phase)
+
+        for phase in range(tiles):
+            if each * phase + 1 < min(each * (phase + 1) + 1, steps - 1):
+                @pl.loop(each * phase + 1, min(each * (phase + 1) + 1, steps - 1))
+                def _(step):
+                    invert(some(tiles, functools.partial(update, step=step - 1, phase=phase)))
+                    next_diag(step)
+                    scale_step(step, phase, a_ref, m_ref, lcat, rcat, pair)
+                    send(step - 1)
+
+        phase = tiles - 1
         last = steps - 1
-        invert(
-            eliminate(last - 1, phase, a_ref, m_ref, lcat, rcat, pair) + product(last - 1, phase) + unscaled_last()
-        )
+
+        @pl.loop(0, tiles)
+        def _(t):
+            trail(t, phase)
+
+        last_rows()
+
+        def finish(t):
+            product(t, last - 1, phase)
+            unscaled(t)
+
+        invert(some(tiles, finish))
         send(last - 1)
         mh, ml = halves(m_ref[...])
-        for t in range(side // tile):
+        for t in range(tiles):
             span = slice(t * tile, (t + 1) * tile)
             x_ref[span, columns(last)] = nt(lcat[span, :], jnp.concatenate([mh, mh, ml], axis=1)).astype(BF16)
         send(last)
@@ -416,7 +437,8 @@
             pltpu.VMEM((side, 3 * NB), BF16),
             pltpu.VMEM((3 * NB, side), BF16),
             pltpu.VMEM((2 * NB, side), BF16),
-            square, square, square,
+            pltpu.VMEM((2 * NB, side), BF16),
+            square, square,
             dma((4,)), dma((lanes,)), dma((lanes,)), dma((4,)),
             dma((steps, lanes)), dma((2, steps)), dma((steps,)),
         ],

time: 97 us -> 105 us (1.082)
  Pallas kernels: 96.2 us -> 104 us
    pallas_call x1, Pallas kernels: 94.3 us -> 103 us  [body(): pl.pallas_call(functools.partial(kernel, lanes), out_shape=jax.ShapeDtype...]
where the time goes in v6:
time: 105 us
  Pallas kernels  104 us (99%)
    pallas_call x1, Pallas kernels, body(): pl.pallas_call(functools.partial(kernel, lanes), out_shape=jax.ShapeDtype...  103 us

profile of v6, /device:TPU:6, one launch (start us, length us, event | category | flops | bytes accessed | tf_op | source)
XLA Modules:
  0.0 105.1 jit_solution(1365762352096155567)
XLA Ops:
  0.6 102.6 %refresh.1.both = bf16[2,128,1024]{2,1,0:T(8,128)(2,1)} custom-call(s32[64]{0:T(128)} %rc_ref.1, s32[64]{0:T(128)} %cc_ref.1, bf16[128,1024]{1,0:T(8,128)(2,1)} %bitcast.5, bf16[128,1024]{1,0:T(8,128)(2,1)} %bitcast.6, bf16[128,1024]{1,0:T(8,128)(2,1)} %bitcast.7), custom_call_target="tpu_custom_call" | custom-call | flops 15032385536 | bytes 6291456 | tf_op jit(solution)/shard_map/refresh/pallas_call | solution.py:428
  103.3 1.8 %hand_on.1 = (bf16[128,1024]{1,0:T(8,128)(2,1)}, bf16[128,1024]{1,0:T(8,128)(2,1)}) custom-call(bf16[2,128,1024]{2,1,0:T(8,128)(2,1)} %refresh.1.both), custom_call_target="tpu_custom_call" | custom-call | tf_op jit(solution)/shard_map/hand_on/pallas_call | solution.py:451

commit v7 on v4

--- a/solution.py
+++ b/solution.py
@@ -180,7 +180,7 @@
 def kernel(
     lanes, rc_ref, cc_ref, g_in, l_in, r_in, out,
     gm, gbuf, pbuf, s_ref, w_ref, x_ref, a_ref, lcat, rcat, pair, m_ref, d_ref,
-    ssem, gsem, psem, osem, xsend, xrecv, xown,
+    relay, ssem, gsem, psem, osem, xsend, xrecv, xown, hsem, fsem,
 ):
     me = lax.axis_index("tensor")
     block = lax.axis_index("fsdp")
@@ -207,11 +207,35 @@
             device_id={"tensor": to}, device_id_type=MESH,
         )
 
+    turn_of = 1 - 2 * lax.rem(block, 2)
+
+    def via(to):
+        return lax.rem(to + lanes // 2 + turn_of + lanes, lanes)
+
+    def handed(kind, src, k):
+        return pltpu.make_async_remote_copy(
+            src_ref=src, dst_ref=relay.at[kind], send_sem=ssem.at[k], recv_sem=hsem.at[kind],
+            device_id={"tensor": lax.rem(me + turn_of + lanes, lanes)}, device_id_type=MESH,
+        )
+
+    def hand_over(kind, dst, sem, to):
+        source = lax.rem(to + lanes // 2, lanes)
+        return pltpu.make_async_remote_copy(
+            src_ref=relay.at[kind], dst_ref=dst.at[rows_of(source)], send_sem=fsem.at[kind], recv_sem=sem.at[source],
+            device_id={"tensor": to}, device_id_type=MESH,
+        )
+
     jobs = (
         (left, gm, gbuf, 0, gsem), (right, gm, gbuf, 1, gsem), (left, l_in, pbuf, 2, psem), (right, r_in, pbuf, 3, psem)
     )
     for to, src, dst, k, sem in jobs:
-        @pl.when(me != to)
+        opposite = me == lax.rem(to + lanes // 2, lanes)
+
+        @pl.when(opposite)
+        def _():
+            handed(k // 2, src, k).start()
+
+        @pl.when((me != to) & jnp.logical_not(opposite))
         def _():
             remote(src, dst, k, sem, to).start()
 
@@ -320,6 +344,16 @@
         @pl.when(me == worker)
         def _():
             begin(which)
+
+    for to in (left, right):
+        @pl.when(me == via(to))
+        def _():
+            parts = ((0, gm, gbuf, gsem, 0), (1, l_in, pbuf, psem, 2))
+            for kind, src, dst, sem, k in parts:
+                handed(kind, src, k).wait_recv()
+                hand_over(kind, dst, sem, to).start()
+            for kind, src, dst, sem, k in parts:
+                hand_over(kind, dst, sem, to).wait_send()
 
     working = (me == left) | (me == right)
     side_of = lax.div(lax.rem(me - left + lanes, lanes), lanes // 2)
@@ -413,8 +447,9 @@
             pltpu.VMEM((3 * NB, side), BF16),
             pltpu.VMEM((2 * NB, side), BF16),
             square, square,
+            pltpu.VMEM((2, rows, side), BF16),
             dma((4,)), dma((lanes,)), dma((lanes,)), dma((4,)),
-            dma((steps, lanes)), dma((2, steps)), dma((steps,)),
+            dma((steps, lanes)), dma((2, steps)), dma((steps,)), dma((2,)), dma((2,)),
         ],
         compiler_params=pltpu.CompilerParams(
             collective_id=0, has_side_effects=True, vmem_limit_bytes=VMEM_LIMIT

time: 97 us -> 91.5 us (0.943)
  Pallas kernels: 96.1 us -> 90.6 us
    pallas_call x1, Pallas kernels: 94.3 us -> 88.8 us  [body(): pl.pallas_call(functools.partial(kernel, lanes), out_shape=jax.ShapeDtype...]
where the time goes in v7:
time: 91.5 us; the launch traced here: 91.3 us
  Pallas kernels  90.6 us (99%)
    pallas_call x1, Pallas kernels, body(): pl.pallas_call(functools.partial(kernel, lanes), out_shape=jax.ShapeDtype...  88.8 us
    pallas_call x1, Pallas kernels, body(): pl.pallas_call(hand_on, out_shape=(part, part), in_specs=[vmem], out_spec...  1.85 us

profile of v7, /device:TPU:6, one launch (start us, length us, event | category | flops | bytes accessed | tf_op | source)
XLA Modules:
  0.0 91.3 jit_solution(2895501226898596790)
XLA Ops:
  0.6 88.8 %refresh.1.both = bf16[2,128,1024]{2,1,0:T(8,128)(2,1)} custom-call(s32[64]{0:T(128)} %rc_ref.1, s32[64]{0:T(128)} %cc_ref.1, bf16[128,1024]{1,0:T(8,128)(2,1)} %bitcast.5, bf16[128,1024]{1,0:T(8,128)(2,1)} %bitcast.6, bf16[128,1024]{1,0:T(8,128)(2,1)} %bitcast.7), custom_call_target="tpu_custom_call" | custom-call | flops 15032385536 | bytes 6291456 | tf_op jit(solution)/shard_map/refresh/pallas_call | solution.py:437
  89.4 1.8 %hand_on.1 = (bf16[128,1024]{1,0:T(8,128)(2,1)}, bf16[128,1024]{1,0:T(8,128)(2,1)}) custom-call(bf16[2,128,1024]{2,1,0:T(8,128)(2,1)} %refresh.1.both), custom_call_target="tpu_custom_call" | custom-call | tf_op jit(solution)/shard_map/hand_on/pallas_call | solution.py:460

commit v8 on v7

--- a/solution.py
+++ b/solution.py
@@ -81,20 +81,20 @@
             flat[n] = flat[n] - low[n] * flat[p]
             for s in range(n + 1, 8):
                 flat[s] = flat[s] - low[s] * flat[p] - high[s] * flat[n]
-        for i in range(r + 1, min(r + 3, count)):
+        for i in range(r + 1, min(r + 4, count)):
             rows[i] = group_update(rows[i], inside, k0, rcp, u, flat)
         scaled = jnp.zeros((8, NB), F32)
         for p in range(8):
             scaled = jnp.where(sub == p, flat[p] * root[p], scaled)
         store(r, jnp.where(lane <= sub + k0, scaled, 0.0))
-        if r + 3 < count:
+        if r + 4 < count:
             high = scaled.astype(BF16).astype(F32)
             low = scaled - high
             zero = jnp.zeros((8, NB), F32)
             left = jnp.concatenate([high, low, high, zero], axis=0).astype(BF16)
             right = jnp.concatenate([high, high, low, zero], axis=0).astype(BF16)
             off = tn(left, right)
-            for i in range(r + 3, count):
+            for i in range(r + 4, count):
                 rows[i] = jnp.where(inside, 0.0, rows[i]) - off[8 * i : 8 * i + 8, :]
         yield
 

time: 91.5 us -> 91.4 us (level)
  no operation moved by 1% of the time
where the time goes in v8:
time: 91.4 us; the launch traced here: 91.2 us
  Pallas kernels  90.6 us (99%)
    pallas_call x1, Pallas kernels, body(): pl.pallas_call(functools.partial(kernel, lanes), out_shape=jax.ShapeDtype...  88.7 us
    pallas_call x1, Pallas kernels, body(): pl.pallas_call(hand_on, out_shape=(part, part), in_specs=[vmem], out_spec...  1.85 us

profile of v8, /device:TPU:6, one launch (start us, length us, event | category | flops | bytes accessed | tf_op | source)
XLA Modules:
  0.0 91.2 jit_solution(12524162810003653927)
XLA Ops:
  0.6 88.7 %refresh.1.both = bf16[2,128,1024]{2,1,0:T(8,128)(2,1)} custom-call(s32[64]{0:T(128)} %rc_ref.1, s32[64]{0:T(128)} %cc_ref.1, bf16[128,1024]{1,0:T(8,128)(2,1)} %bitcast.5, bf16[128,1024]{1,0:T(8,128)(2,1)} %bitcast.6, bf16[128,1024]{1,0:T(8,128)(2,1)} %bitcast.7), custom_call_target="tpu_custom_call" | custom-call | flops 15032385536 | bytes 6291456 | tf_op jit(solution)/shard_map/refresh/pallas_call | solution.py:437
  89.4 1.8 %hand_on.1 = (bf16[128,1024]{1,0:T(8,128)(2,1)}, bf16[128,1024]{1,0:T(8,128)(2,1)}) custom-call(bf16[2,128,1024]{2,1,0:T(8,128)(2,1)} %refresh.1.both), custom_call_target="tpu_custom_call" | custom-call | tf_op jit(solution)/shard_map/hand_on/pallas_call | solution.py:460
